TPU v7x, 512 devices: a whole 4x4x16 slice. The times are simulated.
512 devices in a mesh: tile: 128 (over x, z, core), ch: 4 (over y).
Axes of the slice: x: 4, y: 4, z: 16, core: 2. Of those that a mesh axis runs over, the one named last changes fastest.
Arguments:
- phases: float32 [32, 1024, 16, 128], P('ch', 'tile'), may hold values from 0 to 1
- node_temp: float32 [32768, 128], P('tile'), may hold values from -6 to 6
- column_nodes: int32 [16384], P('tile'), may hold values from 0 to 32767, as said below
- grain_ids: int32 [128, 32], P('tile'), may hold values from 0 to 4095, as said below
- grain_angle: float32 [4096], replicated, may hold values from -3.140625 to 3.140625
- grain_melt: float32 [4096], replicated, may hold values from -1 to 1
- heat_owner: int32 [2048, 1], P('tile'), may hold values from 0 to 127, as said below
- heat_local: int32 [2048], P('tile'), may hold values from 0 to 255
Outputs:
- phases_out: float32 [32, 1024, 16, 128], P('ch', 'tile')
- temp_out: float32 [32768, 128], P('tile')
Inputs may be any that keep to these rules, and one draw needn't show every extreme that they name: `column_nodes`: node ids; of the 128 columns of one tile at most 2 take nodes of one owner (id // 256), and exactly 2 take nodes of that tile's own index. `grain_ids`: the 32 ids of a row are distinct. `heat_owner`: A row of tile t names an owner (t + d) mod 128 with d from -3 to 3; in the rows of one tile index no owner is named more than 4 times, and one owner exactly 4 times.
All inputs are finite; a program needn't handle non-finite values.
Results may differ from a plain program's by a relative error of at most 0.0003.
Values may be sent and summed in bfloat16 or wider, within the bound.
A program may use at most 64 MiB of HBM per device.

v0:
```python
import jax
import jax.numpy as jnp
from jax import lax
from jax.sharding import PartitionSpec as P

STEPS = 2


time_step = 0.1
stiffness = 1.0
interface_energy = 1.0
drive_gain = 3.0
heat_gain = 0.5
depth_diffusion = 0.2
owner_reach = 3


def shifted(shard, axis, by):
    length = lax.axis_size(axis)
    return lax.ppermute(shard, axis, [(i, (i + by) % length) for i in range(length)])


def extended(cells, sides, width):
    for axis, dim in sides:
        count = lax.axis_size(axis)
        ends = count - 1
        head = lax.slice_in_dim(cells, 0, width, axis=dim)
        tail = lax.slice_in_dim(cells, cells.shape[dim] - width, cells.shape[dim], axis=dim)
        cells = jnp.concatenate(
            [
                lax.ppermute(tail, axis, [(i, (i + 1) % count) for i in range(ends)]),
                cells,
                lax.ppermute(head, axis, [((i + 1) % count, i) for i in range(ends)]),
            ],
            axis=dim,
        )
    return cells


def neighbours(values, axis):
    length = values.shape[axis]
    widths = [(0, 0)] * values.ndim
    widths[axis] = (1, 1)
    padded = jnp.pad(values, widths)
    return lax.slice_in_dim(padded, 2, length + 2, axis=axis) + lax.slice_in_dim(
        padded, 0, length, axis=axis
    )


def sideways(values):
    return values[:, 2:] + values[:, :-2]


def middle(values):
    return values[:, 1:-1]


def laplacian(padded):
    along_y = neighbours(padded, 2)
    along_z = neighbours(padded, 3)
    along_yz = neighbours(along_y, 3)
    faces = sideways(padded) + middle(along_y) + middle(along_z)
    edges = sideways(along_y) + sideways(along_z) + middle(along_yz)
    corners = sideways(along_yz)
    return (6.0 * faces + 3.0 * edges + 2.0 * corners - 88.0 * middle(padded)) / 26.0


def coupling(angles):
    spread = angles[..., :, None] - angles[..., None, :]
    count = angles.shape[-1]
    off_diagonal = 1.0 - jnp.eye(count, dtype=jnp.float32)
    return (interface_energy / count * (0.3 + jnp.abs(jnp.sin(spread))) * off_diagonal).astype(
        jnp.bfloat16
    )


def advance(padded, mixing, cell_temp, melts):
    current = middle(padded)
    drive = -drive_gain * (cell_temp[None] - melts[:, None, None, None]) * current * (1.0 - current)
    return current + time_step * (stiffness * laplacian(padded) - mixing + drive)


def pooled_heat(updated, current):
    latent = jnp.sum(updated - current, axis=0)
    planes, across, depth = latent.shape
    return (
        latent.reshape(planes, across // 8, 8, depth)
        .sum(axis=2)
        .reshape(planes * (across // 8), depth)
    )


def conduct(node_temp, heat):
    edged = jnp.pad(node_temp, ((0, 0), (1, 1)), mode="edge")
    return (
        node_temp
        + heat_gain * heat
        + depth_diffusion * (edged[:, 2:] - 2.0 * node_temp + edged[:, :-2])
    )


def slot_numbers(owners, peers):
    member = (owners[:, None] == peers[None, :]).astype(jnp.int32)
    return jnp.sum((jnp.cumsum(member, axis=0) - 1) * member, axis=1)


def on_device(
    phases, node_temp, column_nodes, grain_ids, grain_angle, grain_melt, heat_owner, heat_local
):
    tile_count = lax.axis_size("tile")
    group = lax.axis_index("ch")
    here = lax.axis_index("tile")
    channels, planes, across, depth = phases.shape
    node_rows = node_temp.shape[0]
    columns = column_nodes.shape[0]
    pooled_rows = heat_owner.shape[0]
    near_count = 2 * owner_reach + 1
    fetch_cap = max(2, 2 * columns // tile_count)
    heat_cap = max(2, 2 * pooled_rows // near_count)
    peers = jnp.arange(tile_count, dtype=jnp.int32)
    nearby = jnp.arange(near_count, dtype=jnp.int32)
    owners = column_nodes // node_rows
    fetch_slot = slot_numbers(owners, peers)
    requests = (
        jnp.zeros((tile_count, fetch_cap), jnp.int32)
        .at[owners, fetch_slot]
        .set(column_nodes % node_rows)
    )
    picks = owners * fetch_cap + fetch_slot
    wanted = lax.all_to_all(requests, "tile", split_axis=0, concat_axis=0, tiled=True)
    offsets = (heat_owner[:, 0] - here + owner_reach + tile_count) % tile_count
    heat_slot = slot_numbers(offsets, nearby)
    target_table = (
        jnp.zeros((near_count, heat_cap), jnp.int32).at[offsets, heat_slot].set(heat_local)
    )
    arriving = jnp.stack(
        [shifted(target_table[index], "tile", index - owner_reach) for index in range(near_count)]
    )
    node_ids = jnp.arange(node_rows, dtype=jnp.int32)
    arrival_map = (node_ids[:, None] == arriving.reshape(-1)[None, :]).astype(jnp.float32)
    catalog = jnp.arange(grain_angle.shape[0], dtype=jnp.int32)
    chosen = (grain_ids[0][:, None] == catalog[None, :]).astype(jnp.float32)
    angles = jnp.dot(chosen, grain_angle, precision=lax.Precision.HIGHEST)
    melts = jnp.dot(chosen, grain_melt, precision=lax.Precision.HIGHEST)
    weights = coupling(angles)
    own_weights = lax.dynamic_slice_in_dim(weights, group * channels, channels, 0)
    own_melts = lax.dynamic_slice_in_dim(melts, group * channels, channels, 0)
    for repeat in range(STEPS):
        replies = lax.all_to_all(node_temp[wanted], "tile", split_axis=0, concat_axis=0, tiled=True)
        cell_rows = replies.reshape(-1, depth)[picks]
        cell_temp = cell_rows.reshape(planes, across, depth)
        padded = extended(phases, (("tile", 1),), 1)
        rounded = phases.astype(jnp.bfloat16)
        everyone = lax.all_gather(rounded, "ch", axis=0, tiled=True)
        mixing = jnp.einsum(
            "ij,jxyz->ixyz", own_weights, everyone, preferred_element_type=jnp.float32
        )
        updated = advance(padded, mixing, cell_temp, own_melts)
        pooled = pooled_heat(updated, phases)
        outgoing = (
            jnp.zeros((near_count, heat_cap, depth), jnp.float32).at[offsets, heat_slot].set(pooled)
        )
        incoming = jnp.stack(
            [shifted(outgoing[index], "tile", index - owner_reach) for index in range(near_count)]
        )
        group_heat = jnp.dot(
            arrival_map, incoming.reshape(-1, depth), precision=lax.Precision.HIGHEST
        )
        heat = lax.psum(group_heat, "ch")
        node_temp = conduct(node_temp, heat)
        phases = updated
    return (phases, node_temp)


def solution(mesh):
    placed = (
        P("ch", "tile", None, None),
        P("tile", None),
        P("tile"),
        P("tile", None),
        P(),
        P(),
        P("tile", None),
        P("tile"),
    )
    return jax.shard_map(
        on_device,
        mesh=mesh,
        in_specs=placed,
        out_specs=(P("ch", "tile", None, None), P("tile", None)),
        check_vma=False,
    )
```

profile of v0, /device:TPU:1, one launch (start us, length us, event | category | flops | bytes accessed | tf_op | source)
XLA Modules:
  0.0 306.6 jit_solution(3625755609686488701)
XLA Ops:
  8.4 6.4 %scatter_fusion = s32[128,2]{0,1:T(2,128)S(1)} fusion(s32[128,2]{0,1:T(2,128)S(1)} %broadcast.174, s32[128]{0:T(128)S(1)} %fusion.57, s32[128]{0:T(128)S(1)} %get-tuple-element.45), kind=kCustom, calls=%fused_computation.4 | custom fusion | bytes 2560 | tf_op jit(solution)/shard_map/scatter | solution.py:127
  15.5 20.4 %all-to-all-start = ((s32[128,1,2]{2,1,0:T(1,128)}), s32[128,1,2]{2,1,0:T(1,128)S(1)}, u32[]{:S(2)}, u32[]{:S(2)}) async-start(s32[128,1,2]{2,1,0:T(1,128)} %copy.55), calls=%async_computation | async-start | bytes 131072 | tf_op jit(solution)/shard_map/all_to_all | solution.py:130
  36.3 3.5 %collective-permute-start.1 = (f32[8,1,16,128]{3,0,2,1:T(8,128)S(1)}, f32[8,1,16,128]{3,0,2,1:T(8,128)S(1)}, u32[]{:S(2)}, u32[]{:S(2)}) collective-permute-start(f32[8,1,16,128]{3,0,2,1:T(8,128)S(1)} %get-tuple-element.26), channel_id=1, source_target_pairs={{0,4},{4,8},{8,12},{12,16},{16,20},{20,24},{24,28},{28,32},{32,36}... | collective-permute-start | bytes 196616 | tf_op jit(solution)/shard_map/ppermute | solution.py:31
  39.9 1.9 collective-permute-start
  41.8 1.0 copy.65
  44.2 1.3 scatter_fusion.1
  45.5 5.3 %all-to-all-done = s32[128,1,2]{2,1,0:T(1,128)S(1)} async-done(((s32[128,1,2]{2,1,0:T(1,128)}), s32[128,1,2]{2,1,0:T(1,128)S(1)}, u32[]{:S(2)}, u32[]{:S(2)}) %all-to-all-start) | async-done | bytes 1056 | tf_op jit(solution)/shard_map/all_to_all | solution.py:130
  51.0 1.3 gather_fusion
  52.4 12.2 %all-to-all-start.1 = ((f32[128,2,128]{2,1,0:T(2,128)}), f32[128,2,128]{2,1,0:T(2,128)S(1)}, u32[]{:S(2)}, u32[]{:S(2)}) async-start(f32[128,2,128]{2,1,0:T(2,128)} %bitcast.10), calls=%async_computation.1 | async-start | bytes 262144 | tf_op jit(solution)/shard_map/all_to_all | solution.py:149
  65.0 1.3 fusion.8
  66.7 15.3 %all-to-all-done.1 = f32[128,2,128]{2,1,0:T(2,128)S(1)} async-done(((f32[128,2,128]{2,1,0:T(2,128)}), f32[128,2,128]{2,1,0:T(2,128)S(1)}, u32[]{:S(2)}, u32[]{:S(2)}) %all-to-all-start.1) | async-done | bytes 131104 | tf_op jit(solution)/shard_map/all_to_all | solution.py:149
  82.6 3.5 %subtract_reduce_fusion.1 = (f32[8,16,128]{2,1,0:T(8,128)S(1)}, bf16[8,8,16,128]{3,0,2,1:T(8,128)(2,1)}, f32[8,8,16,128]{3,0,2,1:T(8,128)S(1)}) fusion(f32[8,8,16,128]{3,2,1,0:T(8,128)S(1)} %copy-done.2, f32[8,8,16,128]{3,0,2,1:T(8,128)S(1)} %copy.58, f32[8]{0:T(128)S(1)} %dynamic_slice.7, f32[8,16,128]{2,1,0:T(8,128)S(1)} %bitcast.129, ...), kind=kOutput, calls=%fused_computation.72 | convolution fusion | flops 12306688 | bytes 7869952 | tf_op jit(solution)/shard_map/ij,jxyz->ixyz/dot_general | solution.py:155
  86.2 1.3 scatter_fusion.2
  87.5 4.7 %collective-permute-start.11 = (f32[4,128]{1,0:T(4,128)S(1)}, f32[4,128]{1,0:T(4,128)S(1)}, u32[]{:S(2)}, u32[]{:S(2)}) collective-permute-start(f32[4,128]{1,0:T(4,128)S(1)} %get-tuple-element.44), channel_id=1, source_target_pairs={{0,500},{4,504},{8,508},{12,0},{16,4},{20,8},{24,12},{28,16},{32,2... | collective-permute-start | bytes 6152 | tf_op jit(solution)/shard_map/ppermute | solution.py:20
  92.5 2.7 collective-permute-start.4
  95.2 3.0 collective-permute-start.5
  98.2 3.7 %collective-permute-start.6 = (s32[4]{0:T(128)S(1)}, s32[4]{0:T(128)S(1)}, u32[]{:S(2)}, u32[]{:S(2)}) collective-permute-start(s32[4]{0:T(128)S(1)} %get-tuple-element.14), channel_id=1, source_target_pairs={{0,508},{4,0},{8,4},{12,8},{16,12},{20,16},{24,20},{28,24},{32,28}... | collective-permute-start | bytes 56 | tf_op jit(solution)/shard_map/ppermute | solution.py:20
  102.0 2.2 collective-permute-start.8
  104.2 2.3 collective-permute-start.9
  106.5 2.8 collective-permute-start.10
  109.3 3.0 collective-permute-done.9
  112.3 2.5 collective-permute-done.10
  114.9 3.4 %collective-permute-start.12 = (f32[4,128]{1,0:T(4,128)S(1)}, f32[4,128]{1,0:T(4,128)S(1)}, u32[]{:S(2)}, u32[]{:S(2)}) collective-permute-start(f32[4,128]{1,0:T(4,128)S(1)} %get-tuple-element.43), channel_id=1, source_target_pairs={{0,504},{4,508},{8,0},{12,4},{16,8},{20,12},{24,16},{28,20},{32,24... | collective-permute-start | bytes 6152 | tf_op jit(solution)/shard_map/ppermute | solution.py:20
  118.3 3.5 %collective-permute-start.13 = (f32[4,128]{1,0:T(4,128)S(1)}, f32[4,128]{1,0:T(4,128)S(1)}, u32[]{:S(2)}, u32[]{:S(2)}) collective-permute-start(f32[4,128]{1,0:T(4,128)S(1)} %get-tuple-element.42), channel_id=1, source_target_pairs={{0,508},{4,0},{8,4},{12,8},{16,12},{20,16},{24,20},{28,24},{32,28}... | collective-permute-start | bytes 6152 | tf_op jit(solution)/shard_map/ppermute | solution.py:20
  121.8 2.1 collective-permute-start.15
  123.9 2.0 collective-permute-start.16
  125.9 2.1 collective-permute-start.17
  128.1 3.4 %collective-permute-done.16 = f32[4,128]{1,0:T(4,128)S(1)} collective-permute-done((f32[4,128]{1,0:T(4,128)S(1)}, f32[4,128]{1,0:T(4,128)S(1)}, u32[]{:S(2)}, u32[]{:S(2)}) %collective-permute-start.16) | collective-permute-done | bytes 2080 | tf_op jit(solution)/shard_map/ppermute | solution.py:20
  131.5 2.7 collective-permute-done.17
  136.0 44.1 %all-reduce.9.cloned.1.call-done = f32[256,128]{1,0:T(8,128)} async-done(((f32[256,128]{1,0:T(8,128)}), f32[256,128]{1,0:T(8,128)}) %all-reduce.9.cloned.1.call-update) | async-done | bytes 131088 | tf_op jit(solution)/shard_map/psum | solution.py:169
  180.1 1.1 fusion.38
  181.1 1.3 gather_fusion.2
  182.5 18.9 %all-to-all-start.2 = ((f32[128,2,128]{2,1,0:T(2,128)}), f32[128,2,128]{2,1,0:T(2,128)S(1)}, u32[]{:S(2)}, u32[]{:S(2)}) async-start(f32[128,2,128]{2,1,0:T(2,128)} %bitcast.42), calls=%async_computation.2 | async-start | bytes 262144 | tf_op jit(solution)/shard_map/all_to_all | solution.py:149
  201.4 2.8 collective-permute-start.2
  204.2 2.8 collective-permute-start.3
  209.5 9.2 %all-to-all-done.2 = f32[128,2,128]{2,1,0:T(2,128)S(1)} async-done(((f32[128,2,128]{2,1,0:T(2,128)}), f32[128,2,128]{2,1,0:T(2,128)S(1)}, u32[]{:S(2)}, u32[]{:S(2)}) %all-to-all-start.2) | async-done | bytes 131104 | tf_op jit(solution)/shard_map/all_to_all | solution.py:149
  219.4 2.0 subtract_reduce_fusion
  221.5 1.3 scatter_fusion.3
  222.8 8.0 %collective-permute-start.18 = (f32[4,128]{1,0:T(4,128)S(1)}, f32[4,128]{1,0:T(4,128)S(1)}, u32[]{:S(2)}, u32[]{:S(2)}) collective-permute-start(f32[4,128]{1,0:T(4,128)S(1)} %get-tuple-element.37), channel_id=1, source_target_pairs={{0,500},{4,504},{8,508},{12,0},{16,4},{20,8},{24,12},{28,16},{32,2... | collective-permute-start | bytes 6152 | tf_op jit(solution)/shard_map/ppermute | solution.py:20
  230.9 3.0 collective-permute-start.19
  233.9 2.0 collective-permute-start.20
  235.9 3.6 %collective-permute-start.22 = (f32[4,128]{1,0:T(4,128)S(1)}, f32[4,128]{1,0:T(4,128)S(1)}, u32[]{:S(2)}, u32[]{:S(2)}) collective-permute-start(f32[4,128]{1,0:T(4,128)S(1)} %get-tuple-element.33), channel_id=1, source_target_pairs={{0,4},{4,8},{8,12},{12,16},{16,20},{20,24},{24,28},{28,32},{32,36}... | collective-permute-start | bytes 6152 | tf_op jit(solution)/shard_map/ppermute | solution.py:20
  239.5 2.3 collective-permute-start.23
  241.8 1.9 collective-permute-start.24
  243.8 3.3 %collective-permute-done.23 = f32[4,128]{1,0:T(4,128)S(1)} collective-permute-done((f32[4,128]{1,0:T(4,128)S(1)}, f32[4,128]{1,0:T(4,128)S(1)}, u32[]{:S(2)}, u32[]{:S(2)}) %collective-permute-start.23) | collective-permute-done | bytes 2080 | tf_op jit(solution)/shard_map/ppermute | solution.py:20
  247.1 3.2 %collective-permute-done.24 = f32[4,128]{1,0:T(4,128)S(1)} collective-permute-done((f32[4,128]{1,0:T(4,128)S(1)}, f32[4,128]{1,0:T(4,128)S(1)}, u32[]{:S(2)}, u32[]{:S(2)}) %collective-permute-start.24) | collective-permute-done | bytes 2080 | tf_op jit(solution)/shard_map/ppermute | solution.py:20
  252.2 46.2 %all-reduce.11.cloned.1.call-done = f32[256,128]{1,0:T(8,128)} async-done(((f32[256,128]{1,0:T(8,128)}), f32[256,128]{1,0:T(8,128)}) %all-reduce.11.cloned.1.call-update) | async-done | bytes 131088 | tf_op jit(solution)/shard_map/psum | solution.py:169
  298.4 1.7 fusion.34
  (110 shorter events, 12.7 us)
Async XLA Ops:
  7.2 36.0 %copy-start = (f32[4096]{0:T(1024)S(1)}, f32[4096]{0:T(1024)}, u32[]{:S(2)}) copy-start(f32[4096]{0:T(1024)} %param.13) | copy-start | bytes 49156
  7.2 28.8 %copy-start.2 = (f32[8,8,16,128]{3,2,1,0:T(8,128)S(1)}, f32[8,8,16,128]{3,2,1,0:T(8,128)}, u32[]{:S(2)}) copy-start(f32[8,8,16,128]{3,2,1,0:T(8,128)} %param.8) | copy-start | bytes 1572868
  15.5 35.4 %all-to-all-start = ((s32[128,1,2]{2,1,0:T(1,128)}), s32[128,1,2]{2,1,0:T(1,128)S(1)}, u32[]{:S(2)}, u32[]{:S(2)}) async-start(s32[128,1,2]{2,1,0:T(1,128)} %copy.55), calls=%async_computation | async-start | bytes 131072 | tf_op jit(solution)/shard_map/all_to_all | solution.py:130
  35.9 7.0 %copy-start.4 = (s32[16,1]{0,1:T(1,128)S(1)}, s32[16,1]{0,1:T(1,128)}, u32[]{:S(2)}) copy-start(s32[16,1]{0,1:T(1,128)} %param.14) | copy-start | bytes 196
  35.9 7.3 %copy-start.6 = (s32[1,32]{1,0:T(1,128)S(1)}, s32[1,32]{1,0:T(1,128)}, u32[]{:S(2)}) copy-start(s32[1,32]{1,0:T(1,128)} %param.11) | copy-start | bytes 388
  35.9 7.7 %copy-start.5 = (f32[4096]{0:T(1024)S(1)}, f32[4096]{0:T(1024)}, u32[]{:S(2)}) copy-start(f32[4096]{0:T(1024)} %param.12) | copy-start | bytes 49156
  35.9 46.7 %all-gather.3.cloned.1.call-start = ((), (), s32[]{:S(2)}) async-start(), calls=%async_computation.3 | async-start | bytes 1310720 | tf_op jit(solution)/shard_map/all_gather | solution.py:154
  36.3 7.9 %copy-start.3 = (s32[16]{0:T(128)S(1)}, s32[16]{0:T(128)}, u32[]{:S(2)}) copy-start(s32[16]{0:T(128)} %param.15) | copy-start | bytes 196
  36.3 28.3 %collective-permute-start.1 = (f32[8,1,16,128]{3,0,2,1:T(8,128)S(1)}, f32[8,1,16,128]{3,0,2,1:T(8,128)S(1)}, u32[]{:S(2)}, u32[]{:S(2)}) collective-permute-start(f32[8,1,16,128]{3,0,2,1:T(8,128)S(1)} %get-tuple-element.26), channel_id=1, source_target_pairs={{0,4},{4,8},{8,12},{12,16},{16,20},{20,24},{24,28},{28,32},{32,36}... | collective-permute-start | bytes 196616 | tf_op jit(solution)/shard_map/ppermute | solution.py:31
  39.9 25.1 %collective-permute-start = (f32[8,1,16,128]{3,0,2,1:T(8,128)S(1)}, f32[8,1,16,128]{3,0,2,1:T(8,128)S(1)}, u32[]{:S(2)}, u32[]{:S(2)}) collective-permute-start(f32[8,1,16,128]{3,0,2,1:T(8,128)S(1)} %get-tuple-element.25), channel_id=1, source_target_pairs={{4,0},{8,4},{12,8},{16,12},{20,16},{24,20},{28,24},{32,28},{36,32}... | collective-permute-start | bytes 196616 | tf_op jit(solution)/shard_map/ppermute | solution.py:33
  42.8 8.2 %copy-start.1 = (f32[256,128]{1,0:T(8,128)S(1)}, f32[256,128]{1,0:T(8,128)}, u32[]{:S(2)}) copy-start(f32[256,128]{1,0:T(8,128)} %param.9) | copy-start | bytes 393220
  52.4 29.6 %all-to-all-start.1 = ((f32[128,2,128]{2,1,0:T(2,128)}), f32[128,2,128]{2,1,0:T(2,128)S(1)}, u32[]{:S(2)}, u32[]{:S(2)}) async-start(f32[128,2,128]{2,1,0:T(2,128)} %bitcast.10), calls=%async_computation.1 | async-start | bytes 262144 | tf_op jit(solution)/shard_map/all_to_all | solution.py:149
  64.6 115.5 %all-reduce.9.cloned.1.call-start = ((), (), s32[]{:S(2)}) async-start(), calls=%async_computation.5 | async-start | bytes 262144 | tf_op jit(solution)/shard_map/psum | solution.py:169
  87.5 36.3 %collective-permute-start.11 = (f32[4,128]{1,0:T(4,128)S(1)}, f32[4,128]{1,0:T(4,128)S(1)}, u32[]{:S(2)}, u32[]{:S(2)}) collective-permute-start(f32[4,128]{1,0:T(4,128)S(1)} %get-tuple-element.44), channel_id=1, source_target_pairs={{0,500},{4,504},{8,508},{12,0},{16,4},{20,8},{24,12},{28,16},{32,2... | collective-permute-start | bytes 6152 | tf_op jit(solution)/shard_map/ppermute | solution.py:20
  92.5 9.4 %collective-permute-start.4 = (s32[4]{0:T(128)S(1)}, s32[4]{0:T(128)S(1)}, u32[]{:S(2)}, u32[]{:S(2)}) collective-permute-start(s32[4]{0:T(128)S(1)} %get-tuple-element.16), channel_id=1, source_target_pairs={{0,500},{4,504},{8,508},{12,0},{16,4},{20,8},{24,12},{28,16},{32,2... | collective-permute-start | bytes 56 | tf_op jit(solution)/shard_map/ppermute | solution.py:20
  95.2 9.0 %collective-permute-start.5 = (s32[4]{0:T(128)S(1)}, s32[4]{0:T(128)S(1)}, u32[]{:S(2)}, u32[]{:S(2)}) collective-permute-start(s32[4]{0:T(128)S(1)} %get-tuple-element.15), channel_id=1, source_target_pairs={{0,504},{4,508},{8,0},{12,4},{16,8},{20,12},{24,16},{28,20},{32,24... | collective-permute-start | bytes 56 | tf_op jit(solution)/shard_map/ppermute | solution.py:20
  98.2 8.3 %collective-permute-start.6 = (s32[4]{0:T(128)S(1)}, s32[4]{0:T(128)S(1)}, u32[]{:S(2)}, u32[]{:S(2)}) collective-permute-start(s32[4]{0:T(128)S(1)} %get-tuple-element.14), channel_id=1, source_target_pairs={{0,508},{4,0},{8,4},{12,8},{16,12},{20,16},{24,20},{28,24},{32,28}... | collective-permute-start | bytes 56 | tf_op jit(solution)/shard_map/ppermute | solution.py:20
  102.0 7.3 %collective-permute-start.7 = (s32[4]{0:T(128)S(1)}, s32[4]{0:T(128)S(1)}, u32[]{:S(2)}, u32[]{:S(2)}) collective-permute-start(s32[4]{0:T(128)S(1)} %get-tuple-element.13), channel_id=1, source_target_pairs={{0,0},{4,4},{8,8},{12,12},{16,16},{20,20},{24,24},{28,28},{32,32},... | collective-permute-start | bytes 56 | tf_op jit(solution)/shard_map/ppermute | solution.py:20
  102.0 7.3 %collective-permute-start.8 = (s32[4]{0:T(128)S(1)}, s32[4]{0:T(128)S(1)}, u32[]{:S(2)}, u32[]{:S(2)}) collective-permute-start(s32[4]{0:T(128)S(1)} %get-tuple-element.12), channel_id=1, source_target_pairs={{0,4},{4,8},{8,12},{12,16},{16,20},{20,24},{24,28},{28,32},{32,36}... | collective-permute-start | bytes 56 | tf_op jit(solution)/shard_map/ppermute | solution.py:20
  104.2 8.1 %collective-permute-start.9 = (s32[4]{0:T(128)S(1)}, s32[4]{0:T(128)S(1)}, u32[]{:S(2)}, u32[]{:S(2)}) collective-permute-start(s32[4]{0:T(128)S(1)} %get-tuple-element.11), channel_id=1, source_target_pairs={{0,8},{4,12},{8,16},{12,20},{16,24},{20,28},{24,32},{28,36},{32,40... | collective-permute-start | bytes 56 | tf_op jit(solution)/shard_map/ppermute | solution.py:20
  106.5 8.3 %collective-permute-start.10 = (s32[4]{0:T(128)S(1)}, s32[4]{0:T(128)S(1)}, u32[]{:S(2)}, u32[]{:S(2)}) collective-permute-start(s32[4]{0:T(128)S(1)} %get-tuple-element.10), channel_id=1, source_target_pairs={{0,12},{4,16},{8,20},{12,24},{16,28},{20,32},{24,36},{28,40},{32,4... | collective-permute-start | bytes 56 | tf_op jit(solution)/shard_map/ppermute | solution.py:20
  114.9 11.0 %collective-permute-start.12 = (f32[4,128]{1,0:T(4,128)S(1)}, f32[4,128]{1,0:T(4,128)S(1)}, u32[]{:S(2)}, u32[]{:S(2)}) collective-permute-start(f32[4,128]{1,0:T(4,128)S(1)} %get-tuple-element.43), channel_id=1, source_target_pairs={{0,504},{4,508},{8,0},{12,4},{16,8},{20,12},{24,16},{28,20},{32,24... | collective-permute-start | bytes 6152 | tf_op jit(solution)/shard_map/ppermute | solution.py:20
  118.3 9.8 %collective-permute-start.13 = (f32[4,128]{1,0:T(4,128)S(1)}, f32[4,128]{1,0:T(4,128)S(1)}, u32[]{:S(2)}, u32[]{:S(2)}) collective-permute-start(f32[4,128]{1,0:T(4,128)S(1)} %get-tuple-element.42), channel_id=1, source_target_pairs={{0,508},{4,0},{8,4},{12,8},{16,12},{20,16},{24,20},{28,24},{32,28}... | collective-permute-start | bytes 6152 | tf_op jit(solution)/shard_map/ppermute | solution.py:20
  121.7 6.3 %collective-permute-start.14 = (f32[4,128]{1,0:T(4,128)S(1)}, f32[4,128]{1,0:T(4,128)S(1)}, u32[]{:S(2)}, u32[]{:S(2)}) collective-permute-start(f32[4,128]{1,0:T(4,128)S(1)} %get-tuple-element.41), channel_id=1, source_target_pairs={{0,0},{4,4},{8,8},{12,12},{16,16},{20,20},{24,24},{28,28},{32,32},... | collective-permute-start | bytes 6152 | tf_op jit(solution)/shard_map/ppermute | solution.py:20
  121.8 6.3 %collective-permute-start.15 = (f32[4,128]{1,0:T(4,128)S(1)}, f32[4,128]{1,0:T(4,128)S(1)}, u32[]{:S(2)}, u32[]{:S(2)}) collective-permute-start(f32[4,128]{1,0:T(4,128)S(1)} %get-tuple-element.40), channel_id=1, source_target_pairs={{0,4},{4,8},{8,12},{12,16},{16,20},{20,24},{24,28},{28,32},{32,36}... | collective-permute-start | bytes 6152 | tf_op jit(solution)/shard_map/ppermute | solution.py:20
  123.9 7.6 %collective-permute-start.16 = (f32[4,128]{1,0:T(4,128)S(1)}, f32[4,128]{1,0:T(4,128)S(1)}, u32[]{:S(2)}, u32[]{:S(2)}) collective-permute-start(f32[4,128]{1,0:T(4,128)S(1)} %get-tuple-element.39), channel_id=1, source_target_pairs={{0,8},{4,12},{8,16},{12,20},{16,24},{20,28},{24,32},{28,36},{32,40... | collective-permute-start | bytes 6152 | tf_op jit(solution)/shard_map/ppermute | solution.py:20
  125.9 8.4 %collective-permute-start.17 = (f32[4,128]{1,0:T(4,128)S(1)}, f32[4,128]{1,0:T(4,128)S(1)}, u32[]{:S(2)}, u32[]{:S(2)}) collective-permute-start(f32[4,128]{1,0:T(4,128)S(1)} %get-tuple-element.38), channel_id=1, source_target_pairs={{0,12},{4,16},{8,20},{12,24},{16,28},{20,32},{24,36},{28,40},{32,4... | collective-permute-start | bytes 6152 | tf_op jit(solution)/shard_map/ppermute | solution.py:20
  135.2 84.2 %all-gather.5.cloned.1.call-start = ((), (), s32[]{:S(2)}) async-start(), calls=%async_computation.4 | async-start | bytes 1310720 | tf_op jit(solution)/shard_map/all_gather | solution.py:154
  182.5 36.3 %all-to-all-start.2 = ((f32[128,2,128]{2,1,0:T(2,128)}), f32[128,2,128]{2,1,0:T(2,128)S(1)}, u32[]{:S(2)}, u32[]{:S(2)}) async-start(f32[128,2,128]{2,1,0:T(2,128)} %bitcast.42), calls=%async_computation.2 | async-start | bytes 262144 | tf_op jit(solution)/shard_map/all_to_all | solution.py:149
  201.3 97.0 %all-reduce.11.cloned.1.call-start = ((), (), s32[]{:S(2)}) async-start(), calls=%async_computation.6 | async-start | bytes 262144 | tf_op jit(solution)/shard_map/psum | solution.py:169
  201.4 6.5 %collective-permute-start.2 = (f32[8,1,16,128]{3,0,2,1:T(8,128)S(1)}, f32[8,1,16,128]{3,0,2,1:T(8,128)S(1)}, u32[]{:S(2)}, u32[]{:S(2)}) collective-permute-start(f32[8,1,16,128]{3,0,2,1:T(8,128)S(1)} %get-tuple-element.24), channel_id=1, source_target_pairs={{4,0},{8,4},{12,8},{16,12},{20,16},{24,20},{28,24},{32,28},{36,32}... | collective-permute-start | bytes 196616 | tf_op jit(solution)/shard_map/ppermute | solution.py:33
  204.2 4.4 %collective-permute-start.3 = (f32[8,1,16,128]{3,0,2,1:T(8,128)S(1)}, f32[8,1,16,128]{3,0,2,1:T(8,128)S(1)}, u32[]{:S(2)}, u32[]{:S(2)}) collective-permute-start(f32[8,1,16,128]{3,0,2,1:T(8,128)S(1)} %get-tuple-element.23), channel_id=1, source_target_pairs={{0,4},{4,8},{8,12},{12,16},{16,20},{20,24},{24,28},{28,32},{32,36}... | collective-permute-start | bytes 196616 | tf_op jit(solution)/shard_map/ppermute | solution.py:31
  222.8 16.7 %collective-permute-start.18 = (f32[4,128]{1,0:T(4,128)S(1)}, f32[4,128]{1,0:T(4,128)S(1)}, u32[]{:S(2)}, u32[]{:S(2)}) collective-permute-start(f32[4,128]{1,0:T(4,128)S(1)} %get-tuple-element.37), channel_id=1, source_target_pairs={{0,500},{4,504},{8,508},{12,0},{16,4},{20,8},{24,12},{28,16},{32,2... | collective-permute-start | bytes 6152 | tf_op jit(solution)/shard_map/ppermute | solution.py:20
  230.9 10.9 %collective-permute-start.19 = (f32[4,128]{1,0:T(4,128)S(1)}, f32[4,128]{1,0:T(4,128)S(1)}, u32[]{:S(2)}, u32[]{:S(2)}) collective-permute-start(f32[4,128]{1,0:T(4,128)S(1)} %get-tuple-element.36), channel_id=1, source_target_pairs={{0,504},{4,508},{8,0},{12,4},{16,8},{20,12},{24,16},{28,20},{32,24... | collective-permute-start | bytes 6152 | tf_op jit(solution)/shard_map/ppermute | solution.py:20
  233.9 9.8 %collective-permute-start.20 = (f32[4,128]{1,0:T(4,128)S(1)}, f32[4,128]{1,0:T(4,128)S(1)}, u32[]{:S(2)}, u32[]{:S(2)}) collective-permute-start(f32[4,128]{1,0:T(4,128)S(1)} %get-tuple-element.35), channel_id=1, source_target_pairs={{0,508},{4,0},{8,4},{12,8},{16,12},{20,16},{24,20},{28,24},{32,28}... | collective-permute-start | bytes 6152 | tf_op jit(solution)/shard_map/ppermute | solution.py:20
  235.9 7.9 %collective-permute-start.21 = (f32[4,128]{1,0:T(4,128)S(1)}, f32[4,128]{1,0:T(4,128)S(1)}, u32[]{:S(2)}, u32[]{:S(2)}) collective-permute-start(f32[4,128]{1,0:T(4,128)S(1)} %get-tuple-element.34), channel_id=1, source_target_pairs={{0,0},{4,4},{8,8},{12,12},{16,16},{20,20},{24,24},{28,28},{32,32},... | collective-permute-start | bytes 6152 | tf_op jit(solution)/shard_map/ppermute | solution.py:20
  235.9 7.9 %collective-permute-start.22 = (f32[4,128]{1,0:T(4,128)S(1)}, f32[4,128]{1,0:T(4,128)S(1)}, u32[]{:S(2)}, u32[]{:S(2)}) collective-permute-start(f32[4,128]{1,0:T(4,128)S(1)} %get-tuple-element.33), channel_id=1, source_target_pairs={{0,4},{4,8},{8,12},{12,16},{16,20},{20,24},{24,28},{28,32},{32,36}... | collective-permute-start | bytes 6152 | tf_op jit(solution)/shard_map/ppermute | solution.py:20
  239.5 7.6 %collective-permute-start.23 = (f32[4,128]{1,0:T(4,128)S(1)}, f32[4,128]{1,0:T(4,128)S(1)}, u32[]{:S(2)}, u32[]{:S(2)}) collective-permute-start(f32[4,128]{1,0:T(4,128)S(1)} %get-tuple-element.32), channel_id=1, source_target_pairs={{0,8},{4,12},{8,16},{12,20},{16,24},{20,28},{24,32},{28,36},{32,40... | collective-permute-start | bytes 6152 | tf_op jit(solution)/shard_map/ppermute | solution.py:20
  241.8 8.5 %collective-permute-start.24 = (f32[4,128]{1,0:T(4,128)S(1)}, f32[4,128]{1,0:T(4,128)S(1)}, u32[]{:S(2)}, u32[]{:S(2)}) collective-permute-start(f32[4,128]{1,0:T(4,128)S(1)} %get-tuple-element.31), channel_id=1, source_target_pairs={{0,12},{4,16},{8,20},{12,24},{16,28},{20,32},{24,36},{28,40},{32,4... | collective-permute-start | bytes 6152 | tf_op jit(solution)/shard_map/ppermute | solution.py:20
Sparse Core Ops, SparseCore 0:
  43.0 35.1 all-gather.2
  135.3 44.7 all-reduce.8
  182.9 35.2 all-gather.4
  251.3 46.9 all-reduce.10
where the time goes:
time: 309 us; the launch traced here: 307 us
  waiting for transfers between devices  141 us (46%)
  starting transfers between devices  118 us (38%)
  local copies, waits for them, and re-layouts  18.6 us (6%)
  between operations  14.5 us (5%)
  matrix products  8.07 us (3%)
  other arithmetic  7 us (2%)
    psum x2, waiting for transfers between devices, on_device(): heat = lax.psum(group_heat, 'ch')  90.2 us
    ppermute x21, starting transfers between devices, shifted(): lax.ppermute(shard, axis, [(i, (i + by) % length) for i in range(length)])  55.2 us
    all_to_all x2, starting transfers between devices, on_device(): lax.all_to_all(node_temp[wanted], 'tile', split_axis=0, concat_axis=0, ti...  31 us
    all_to_all x2, waiting for transfers between devices, on_device(): lax.all_to_all(node_temp[wanted], 'tile', split_axis=0, concat_axis=0, ti...  24.5 us
    all_to_all x1, starting transfers between devices, on_device(): lax.all_to_all(requests, 'tile', split_axis=0, concat_axis=0, tiled=True)  20.4 us
    ppermute x21, waiting for transfers between devices, shifted(): lax.ppermute(shard, axis, [(i, (i + by) % length) for i in range(length)])  18.2 us
    scatter x1, local copies, waits for them, and re-layouts, on_device(): requests = jnp.zeros((tile_count, fetch_cap), jnp.int32).at[owners, fetch...  6.37 us
    ppermute x2, starting transfers between devices, extended(): lax.ppermute(tail, axis, [(i, (i + 1) % count) for i in range(ends)])  6.3 us
  transfers between devices with their start and end apart: 32, of which 13 were waited for; matrix products, arithmetic and copies ran while one was open for 4% of the time, Pallas kernels for 0%

commit v1 on v0

v1 whole, which is shorter than its diff:
```python
import functools

import jax
import jax.numpy as jnp
from jax import lax
from jax.experimental import pallas as pl
from jax.experimental.pallas import tpu as pltpu
from jax.sharding import PartitionSpec as P

STEPS = 2
MESH = pl.DeviceIdType.MESH
F32 = jnp.float32
BF16 = jnp.bfloat16

time_step = 0.1
interface_energy = 1.0
drive_gain = 3.0
heat_gain = 0.5
depth_diffusion = 0.2

TILES = 128
GROUPS = 4
BLOCK = TILES // GROUPS
SLOTS = 2
REACH = 3
NEAR = 2 * REACH + 1
HEAT_SLOTS = 4
CH = 8
SLOT_ALL = 32
PX = 8
PY = 16
NZ = 128
COLS = PX * PY
NODES = 256
POOL = 16
FAR = BLOCK * SLOTS
HEAT_ROWS = NEAR * HEAT_SLOTS
HEAT_PAD = 32


def iota(shape, dim):
    return lax.broadcasted_iota(jnp.int32, shape, dim)


def dot(a, b):
    return jnp.dot(a, b, preferred_element_type=F32)


def thirds(value):
    high = value.astype(BF16)
    rest = value - high.astype(F32)
    mid = rest.astype(BF16)
    low = (rest - mid.astype(F32)).astype(BF16)
    return high, mid, low


def pick(onehot, value):
    high, mid, low = thirds(value)
    return dot(onehot, high) + (dot(onehot, mid) + dot(onehot, low))


def beside(values):
    rows, lanes = values.shape
    lane = iota((rows, lanes), 1)
    up = jnp.where(lane == lanes - 1, 0.0, pltpu.roll(values, lanes - 1, 1))
    down = jnp.where(lane == 0, 0.0, pltpu.roll(values, 1, 1))
    return up + down


def across(values):
    rows, lanes = values.shape
    place = iota((rows, lanes), 0) % PY
    up = jnp.where(place == PY - 1, 0.0, pltpu.roll(values, rows - 1, 0))
    down = jnp.where(place == 0, 0.0, pltpu.roll(values, 1, 0))
    return up + down


def laplacian(padded):
    flat = padded.reshape((PX + 2) * PY, NZ)
    along_y = across(flat)
    inner = (6.0 * along_y - 88.0 * flat) + beside(6.0 * flat + 3.0 * along_y)
    outer = (6.0 * flat + 3.0 * along_y) + beside(3.0 * flat + 2.0 * along_y)
    total = inner[PY:-PY] + (outer[2 * PY :] + outer[: -2 * PY])
    return total * (1.0 / 26.0)


def conduct(rows):
    lane = iota(rows.shape, 1)
    up = jnp.where(lane == NZ - 1, rows, pltpu.roll(rows, NZ - 1, 1))
    down = jnp.where(lane == 0, rows, pltpu.roll(rows, 1, 1))
    return rows + depth_diffusion * (up - 2.0 * rows + down)


def kernel(
    phases_hbm, temp_hbm, columns_hbm, grains_hbm, angle_hbm, melt_hbm, owner_hbm, local_hbm,
    phases_out, temp_out,
    cells, cells2, static, static2, mixed, gathered, gathered2,
    temp, columns, grains, angles, melts, owners, locals_,
    req_out, req_in, rows_out, rows_in, rows_out2, rows_in2, share, share2,
    heat_out, heat_in, heat_out2, heat_in2, target_out, target_in,
    own_v, all_v, all_v2, flat, heat_flat, final_temp,
    load_sem, send_sem, recv_sem,
):
    tile = lax.axis_index("tile")
    group = lax.axis_index("ch")
    block = tile // BLOCK
    place = tile % BLOCK
    partner = (group + GROUPS - block) % GROUPS
    inside = partner == block

    def far_device(index):
        return {"tile": partner * BLOCK + index, "ch": group}

    def near_device(offset, turn):
        return {"tile": (tile + offset + (TILES - REACH)) % TILES, "ch": (group + turn) % GROUPS}

    barrier = pltpu.get_barrier_semaphore()

    def greet_far(index, _):
        @pl.when(jnp.logical_or(jnp.logical_not(inside), index != place))
        def _():
            pl.semaphore_signal(barrier, inc=1, device_id=far_device(index), device_id_type=MESH)

        return 0

    def greet_near(index, _):
        offset, turn = index // GROUPS, index % GROUPS

        @pl.when(jnp.logical_or(offset != REACH, turn != 0))
        def _():
            pl.semaphore_signal(
                barrier, inc=1, device_id=near_device(offset, turn), device_id_type=MESH
            )

        return 0

    lax.fori_loop(0, BLOCK, greet_far, 0)
    lax.fori_loop(0, NEAR * GROUPS, greet_near, 0)

    loads = [
        pltpu.make_async_copy(phases_hbm, cells.at[:, pl.ds(1, PX)], load_sem.at[0]),
        pltpu.make_async_copy(temp_hbm, temp, load_sem.at[1]),
        pltpu.make_async_copy(columns_hbm, columns, load_sem.at[2]),
        pltpu.make_async_copy(grains_hbm, grains, load_sem.at[3]),
        pltpu.make_async_copy(angle_hbm, angles, load_sem.at[4]),
        pltpu.make_async_copy(melt_hbm, melts, load_sem.at[5]),
        pltpu.make_async_copy(owner_hbm, owners, load_sem.at[6]),
        pltpu.make_async_copy(local_hbm, locals_, load_sem.at[7]),
    ]
    for load in loads:
        load.start()
    for load in loads:
        load.wait()

    wanted = jnp.broadcast_to(columns[...].astype(F32), (COLS, COLS))
    wanted_down = wanted.T
    wanted_i = wanted.astype(jnp.int32)
    wanted_down_i = wanted_down.astype(jnp.int32)
    owner_over = wanted_i // NODES
    owner_down = wanted_down_i // NODES
    local_down = (wanted_down_i % NODES).astype(F32)
    down, over = iota((COLS, COLS), 0), iota((COLS, COLS), 1)
    same = owner_over == owner_down
    slot_over = jnp.sum(jnp.where(same & (down < over), 1.0, 0.0), axis=0, keepdims=True)
    slot_down = jnp.sum(jnp.where(same & (over < down), 1.0, 0.0), axis=1, keepdims=True)
    key_over = owner_over[:1] * SLOTS + slot_over.astype(jnp.int32)
    key_down = owner_down[:, :1] * SLOTS + slot_down.astype(jnp.int32)
    ask = jnp.where(iota((FAR, COLS), 0) + partner * FAR == key_over, 1.0, 0.0).astype(BF16)
    flat[pl.ds(0, FAR), :] = dot(ask, local_down.astype(BF16))
    for index in range(BLOCK):
        req_out[index] = flat[pl.ds(index * SLOTS, SLOTS), :]
    key_lane = iota((COLS, FAR), 1)
    take_own = jnp.where(key_lane + partner * FAR == key_down, 1.0, 0.0).astype(BF16)
    lane_all = iota((COLS, GROUPS * FAR), 1)
    lane_block = (lane_all // FAR + GROUPS - block) % GROUPS
    take_all = jnp.where(
        lane_block * FAR + lane_all % FAR == key_down, 1.0, 0.0
    ).astype(BF16)

    row_down, lane = iota((POOL, COLS), 0), iota((POOL, COLS), 1)
    off_down = jnp.zeros((POOL, COLS), jnp.int32)
    off_over = jnp.zeros((POOL, COLS), jnp.int32)
    local_rows = jnp.zeros((POOL, NZ), jnp.int32)
    for row in range(POOL):
        off = (owners[row] - tile + (REACH + TILES)) % TILES
        off_down = jnp.where(row_down == row, off, off_down)
        off_over = jnp.where(lane // 8 == row, off, off_over)
        local_rows = jnp.where(row_down == row, locals_[row], local_rows)
    earlier = jnp.where((off_down == off_over) & (row_down < lane // 8), 1.0, 0.0)
    heat_slot = jnp.sum(earlier, axis=0, keepdims=True).astype(jnp.int32)
    heat_key = off_over[:1] * HEAT_SLOTS + heat_slot
    spread = iota((HEAT_PAD, COLS), 0) == heat_key
    pool_pick = jnp.where(spread, 1.0, 0.0).astype(BF16)
    row_of = jnp.where(iota((COLS, POOL), 0) == 8 * iota((COLS, POOL), 1), 1.0, 0.0).astype(BF16)
    row_pick = dot(pool_pick, row_of).astype(BF16)
    flat[pl.ds(0, HEAT_PAD), :] = dot(row_pick, local_rows.astype(F32).astype(BF16))
    for offset in range(NEAR):
        target_out[offset] = flat[pl.ds(offset * HEAT_SLOTS, HEAT_SLOTS), :]

    def first_look(channel, total):
        now = cells[channel, pl.ds(1, PX)]
        gathered[group, channel] = now.astype(BF16)
        return total + (now - now * now)

    total = lax.fori_loop(0, CH, first_look, jnp.zeros((PX, PY, NZ), F32))
    total = (time_step * drive_gain) * total.reshape(COLS, NZ)
    own_v[0] = total
    all_v[0] = total

    pl.semaphore_wait(
        barrier, NEAR * GROUPS - 1 + jnp.where(inside, BLOCK - 1, BLOCK).astype(jnp.int32)
    )

    def far_copy(source, target, index, number):
        return pltpu.make_async_remote_copy(
            src_ref=source.at[index],
            dst_ref=target.at[place],
            send_sem=send_sem.at[number],
            recv_sem=recv_sem.at[number],
            device_id=far_device(index),
            device_id_type=MESH,
        )

    def far_send(source, target, number):
        def one(index, _):
            @pl.when(jnp.logical_or(jnp.logical_not(inside), index != place))
            def _():
                far_copy(source, target, index, number).start()

            return 0

        lax.fori_loop(0, BLOCK, one, 0)

        @pl.when(inside)
        def _():
            target[place] = source[place]

    def far_done(buffer, sem, number):
        @pl.when(inside)
        def _():
            part = buffer.at[pl.ds(0, BLOCK - 1)]
            pltpu.make_async_copy(part, part, sem.at[number]).wait()

        @pl.when(jnp.logical_not(inside))
        def _():
            pltpu.make_async_copy(buffer, buffer, sem.at[number]).wait()

    def heat_send(source, target, number):
        def one(index, _):
            offset, turn = index // GROUPS, index % GROUPS

            @pl.when(jnp.logical_or(offset != REACH, turn != 0))
            def _():
                pltpu.make_async_remote_copy(
                    src_ref=source.at[offset],
                    dst_ref=target.at[offset * GROUPS + group],
                    send_sem=send_sem.at[number],
                    recv_sem=recv_sem.at[number],
                    device_id=near_device(offset, turn),
                    device_id_type=MESH,
                ).start()

            return 0

        lax.fori_loop(0, NEAR * GROUPS, one, 0)
        target[REACH * GROUPS + group] = source[REACH]

    def heat_done(buffer, sem, number):
        part = buffer.at[pl.ds(0, NEAR * GROUPS - 1)]
        pltpu.make_async_copy(part, part, sem.at[number]).wait()

    def target_send(number):
        def one(offset, _):
            @pl.when(offset != REACH)
            def _():
                pltpu.make_async_remote_copy(
                    src_ref=target_out.at[offset],
                    dst_ref=target_in.at[offset],
                    send_sem=send_sem.at[number],
                    recv_sem=recv_sem.at[number],
                    device_id=near_device(offset, 0),
                    device_id_type=MESH,
                ).start()

            return 0

        lax.fori_loop(0, NEAR, one, 0)
        target_in[REACH] = target_out[REACH]

    def target_done(buffer, sem, number):
        part = buffer.at[pl.ds(0, NEAR - 1)]
        pltpu.make_async_copy(part, part, sem.at[number]).wait()

    def group_copies(source_of, target_of, number):
        return [
            pltpu.make_async_remote_copy(
                src_ref=source_of(turn),
                dst_ref=target_of(turn),
                send_sem=send_sem.at[number + turn],
                recv_sem=recv_sem.at[number + turn],
                device_id=near_device(REACH, turn),
                device_id_type=MESH,
            )
            for turn in range(1, GROUPS)
        ]

    def halo_copies(buffer, number):
        return [
            pltpu.make_async_remote_copy(
                src_ref=buffer.at[:, 1],
                dst_ref=buffer.at[:, PX + 1],
                send_sem=send_sem.at[number],
                recv_sem=recv_sem.at[number],
                device_id=near_device(REACH - 1, 0),
                device_id_type=MESH,
            ),
            pltpu.make_async_remote_copy(
                src_ref=buffer.at[:, PX],
                dst_ref=buffer.at[:, 0],
                send_sem=send_sem.at[number + 1],
                recv_sem=recv_sem.at[number + 1],
                device_id=near_device(REACH + 1, 0),
                device_id_type=MESH,
            ),
        ]

    REQ, ROWS, ROWS2, HEAT, HEAT2, TARGET = 0, 1, 2, 3, 4, 5
    HALO, HALO2 = 6, 8
    GATHER, GATHER2, SHARE, SHARE2, VEE, VEE2 = 10, 14, 18, 22, 26, 30

    far_send(req_out, req_in, REQ)
    target_send(TARGET)
    halos = halo_copies(cells, HALO)
    vees = group_copies(lambda turn: own_v.at[0], lambda turn: all_v.at[turn], VEE)
    gathers = group_copies(
        lambda turn: gathered.at[group], lambda turn: gathered.at[group], GATHER
    )
    for copy in halos + vees + gathers:
        copy.start()

    angle_down = jnp.zeros((SLOT_ALL, NZ), F32)
    angle_over = jnp.zeros((SLOT_ALL, NZ), F32)
    slot_row, slot_lane = iota((SLOT_ALL, NZ), 0), iota((SLOT_ALL, NZ), 1)
    for slot in range(SLOT_ALL):
        angle = angles[grains[slot]]
        angle_down = jnp.where(slot_row == slot, angle, angle_down)
        angle_over = jnp.where(slot_lane == slot, angle, angle_over)
    strength = interface_energy / SLOT_ALL * (0.3 + jnp.abs(jnp.sin(angle_down - angle_over)))
    strength = jnp.where((slot_row != slot_lane) & (slot_lane < SLOT_ALL), strength, 0.0)
    strength = strength.astype(BF16)
    column_sums = jnp.sum(strength.astype(F32), axis=0, keepdims=True)
    own_row = iota((COLS, SLOT_ALL), 0) // PY + group * CH
    choose = jnp.where(own_row == iota((COLS, SLOT_ALL), 1), 1.0, 0.0).astype(BF16)
    tall = dot(choose, strength).astype(BF16)
    wide_shape = (NZ, SLOT_ALL * PY)
    widen = jnp.where(iota(wide_shape, 0) == iota(wide_shape, 1) // PY, 1.0, 0.0).astype(BF16)
    weights = dot(tall, widen)
    weights = jnp.where(iota(wide_shape, 0) % PY == iota(wide_shape, 1) % PY, weights, 0.0)
    weights = weights.astype(BF16)

    def melt_of(channel):
        return melts[grains[group * CH + channel]]

    def sum_of(channel):
        lanes = iota((1, NZ), 1) == group * CH + channel
        return jnp.sum(jnp.where(lanes, column_sums, 0.0), axis=1, keepdims=True)

    def stencil(buffer, kept):
        @pl.when(tile == 0)
        def _():
            buffer[:, 0] = jnp.zeros((CH, PY, NZ), F32)

        @pl.when(tile == TILES - 1)
        def _():
            buffer[:, PX + 1] = jnp.zeros((CH, PY, NZ), F32)

        def one(channel, total):
            padded = buffer[channel]
            now = padded[1:-1].reshape(COLS, NZ)
            gain = time_step * laplacian(padded)
            gain = gain + (melt_of(channel) * (time_step * drive_gain)) * (now - now * now)
            kept[channel] = now + gain
            rounded = now.astype(BF16).astype(F32)
            return total + (gain - (time_step * sum_of(channel)) * rounded)

        return lax.fori_loop(0, CH, one, jnp.zeros((COLS, NZ), F32))

    def mix(buffer):
        for plane in range(PX):
            right = buffer[:, :, plane].reshape(SLOT_ALL * PY, NZ)
            mixed[:, plane] = dot(weights, right).reshape(CH, PY, NZ)

    for copy in halos:
        copy.wait_recv()
    own_u = stencil(cells, static)

    far_done(req_in, recv_sem, REQ)
    for index in range(BLOCK):
        flat[pl.ds(index * SLOTS, SLOTS), :] = req_in[index]
    asked = flat[pl.ds(0, FAR), :].astype(jnp.int32)
    asked = jnp.concatenate([asked, asked], axis=1)
    serve = jnp.where(asked == iota((FAR, NODES), 1), 1.0, 0.0).astype(BF16)

    def spread_rows(values, out):
        flat[pl.ds(0, FAR), :] = values
        for index in range(BLOCK):
            out[index] = flat[pl.ds(index * SLOTS, SLOTS), :]

    def collect_rows(buffer, kept):
        for index in range(BLOCK):
            kept[0, pl.ds(index * SLOTS, SLOTS), :] = buffer[index]

    spread_rows(pick(serve, temp[...]), rows_out)
    far_send(rows_out, rows_in, ROWS)

    target_done(target_in, recv_sem, TARGET)
    heat_flat[...] = jnp.full((HEAT_PAD, NZ), -1.0, F32)
    for offset in range(NEAR):
        heat_flat[pl.ds(offset * HEAT_SLOTS, HEAT_SLOTS), :] = target_in[offset]
    aims = heat_flat[...].astype(jnp.int32)
    aims = jnp.concatenate([aims, jnp.full((NZ - HEAT_PAD, NZ), -1, jnp.int32)], axis=0)
    low = jnp.where(aims == iota((NZ, NZ), 1), 1.0, 0.0).T
    high = jnp.where(aims == iota((NZ, NZ), 1) + NZ, 1.0, 0.0).T
    scatter = jnp.concatenate([low, high], axis=0)[:, :HEAT_PAD].astype(BF16)
    relay = dot(serve, scatter).astype(BF16)
    warm = conduct(temp[...])
    warm_rows = pick(serve, warm)
    heat_flat[...] = jnp.zeros((HEAT_PAD, NZ), F32)

    def arrived_heat(buffer):
        for offset in range(NEAR):
            parts = [buffer[offset * GROUPS + turn] for turn in range(GROUPS)]
            heat_flat[pl.ds(offset * HEAT_SLOTS, HEAT_SLOTS), :] = (parts[0] + parts[1]) + (
                parts[2] + parts[3]
            )
        return heat_flat[...]

    def send_heat(kept, own_part, vee, out, target, number):
        mine = pick(take_own, kept[0])
        amount = own_part - mine * vee
        flat[pl.ds(0, HEAT_PAD), :] = pick(pool_pick, amount)
        for offset in range(NEAR):
            out[offset] = flat[pl.ds(offset * HEAT_SLOTS, HEAT_SLOTS), :]
        heat_send(out, target, number)

    def share_copies(buffer, number):
        return group_copies(lambda turn: buffer.at[0], lambda turn: buffer.at[turn], number)

    turn_of = (group + GROUPS - lane_all // FAR) % GROUPS
    del turn_of
    take_turn = jnp.where(
        (((group + GROUPS - lane_all // FAR) % GROUPS + GROUPS - block) % GROUPS) * FAR
        + lane_all % FAR
        == key_down,
        1.0,
        0.0,
    ).astype(BF16)
    del take_all

    for copy in vees:
        copy.wait_recv()
    vee = (all_v[0] + all_v[1]) + (all_v[2] + all_v[3])

    far_done(rows_in, recv_sem, ROWS)
    collect_rows(rows_in, share)
    send_heat(share, own_u, vee, heat_out, heat_in, HEAT)
    shares = share_copies(share, SHARE)
    for copy in shares:
        copy.start()

    for copy in gathers:
        copy.wait_recv()
    mix(gathered)
    for copy in shares:
        copy.wait_recv()

    def all_rows(kept):
        return pick(take_turn, kept[...].reshape(GROUPS * FAR, NZ))

    cell_temp = all_rows(share)

    def update(channel, total):
        now = cells[channel, pl.ds(1, PX)].reshape(COLS, NZ)
        change = (time_step * drive_gain) * cell_temp * (now - now * now)
        mixing = mixed[channel].reshape(COLS, NZ)
        new = static[channel] - time_step * mixing - change
        shaped = new.reshape(PX, PY, NZ)
        cells2[channel, pl.ds(1, PX)] = shaped
        gathered2[group, channel] = shaped.astype(BF16)
        return total + (new - new * new)

    total = lax.fori_loop(0, CH, update, jnp.zeros((COLS, NZ), F32))
    total = (time_step * drive_gain) * total
    own_v[1] = total
    all_v2[0] = total
    halos2 = halo_copies(cells2, HALO2)
    vees2 = group_copies(lambda turn: own_v.at[1], lambda turn: all_v2.at[turn], VEE2)
    gathers2 = group_copies(
        lambda turn: gathered2.at[group], lambda turn: gathered2.at[group], GATHER2
    )
    for copy in halos2 + vees2 + gathers2:
        copy.start()

    heat_done(heat_in, recv_sem, HEAT)
    arrived = arrived_heat(heat_in)
    spread_rows(warm_rows + heat_gain * pick(relay, arrived), rows_out2)
    far_send(rows_out2, rows_in2, ROWS2)
    final_temp[...] = conduct(warm + heat_gain * pick(scatter, arrived))

    for copy in halos2:
        copy.wait_recv()
    own_u2 = stencil(cells2, static2)
    for copy in vees2:
        copy.wait_recv()
    vee2 = (all_v2[0] + all_v2[1]) + (all_v2[2] + all_v2[3])

    far_done(rows_in2, recv_sem, ROWS2)
    collect_rows(rows_in2, share2)
    send_heat(share2, own_u2, vee2, heat_out2, heat_in2, HEAT2)
    shares2 = share_copies(share2, SHARE2)
    for copy in shares2:
        copy.start()

    for copy in gathers2:
        copy.wait_recv()
    mix(gathered2)
    for copy in shares2:
        copy.wait_recv()
    cell_temp2 = all_rows(share2)

    def finish(channel, _):
        now = cells2[channel, pl.ds(1, PX)].reshape(COLS, NZ)
        change = (time_step * drive_gain) * cell_temp2 * (now - now * now)
        mixing = mixed[channel].reshape(COLS, NZ)
        new = static2[channel] - time_step * mixing - change
        static2[channel] = new
        return 0

    lax.fori_loop(0, CH, finish, 0)
    store = pltpu.make_async_copy(static2, phases_out, load_sem.at[0])
    store.start()

    heat_done(heat_in2, recv_sem, HEAT2)
    arrived = arrived_heat(heat_in2)
    final_temp[...] = final_temp[...] + heat_gain * pick(scatter, arrived)
    store_temp = pltpu.make_async_copy(final_temp, temp_out, load_sem.at[1])
    store_temp.start()

    far_done(req_out, send_sem, REQ)
    far_done(rows_out, send_sem, ROWS)
    far_done(rows_out2, send_sem, ROWS2)
    heat_done(heat_in, send_sem, HEAT)
    heat_done(heat_in2, send_sem, HEAT2)
    target_done(target_out, send_sem, TARGET)
    for copy in halos + vees + gathers + shares + halos2 + vees2 + gathers2 + shares2:
        copy.wait_send()
    store.wait()
    store_temp.wait()


def on_device(
    phases, node_temp, column_nodes, grain_ids, grain_angle, grain_melt, heat_owner, heat_local
):
    anywhere = pl.BlockSpec(memory_space=pl.ANY)
    vmem, smem = pltpu.VMEM, pltpu.SMEM
    gathered = vmem((GROUPS, CH, PX, PY, NZ), BF16)
    padded = vmem((CH, PX + 2, PY, NZ), F32)
    flat_cells = vmem((CH, COLS, NZ), F32)
    far_rows = vmem((BLOCK, SLOTS, NZ), F32)
    shared = vmem((GROUPS, FAR, NZ), F32)
    heat_out = vmem((NEAR, HEAT_SLOTS, NZ), F32)
    heat_in = vmem((NEAR * GROUPS, HEAT_SLOTS, NZ), F32)
    field = vmem((GROUPS, COLS, NZ), F32)
    new, temp = pl.pallas_call(
        kernel,
        out_shape=(
            jax.ShapeDtypeStruct((CH, COLS, NZ), F32),
            jax.ShapeDtypeStruct(node_temp.shape, F32),
        ),
        in_specs=[anywhere] * 8,
        out_specs=(anywhere, anywhere),
        scratch_shapes=[
            padded, padded, flat_cells, flat_cells, vmem((CH, PX, PY, NZ), F32), gathered, gathered,
            vmem((NODES, NZ), F32), vmem((1, COLS), jnp.int32), smem((SLOT_ALL,), jnp.int32),
            smem((grain_angle.shape[0],), F32), smem((grain_melt.shape[0],), F32),
            smem((POOL,), jnp.int32), smem((POOL,), jnp.int32),
            far_rows, far_rows, far_rows, far_rows, far_rows, far_rows, shared, shared,
            heat_out, heat_in, heat_out, heat_in, heat_out, heat_out,
            vmem((2, COLS, NZ), F32), field, field, vmem((FAR, NZ), F32), vmem((HEAT_PAD, NZ), F32),
            vmem((NODES, NZ), F32),
            pltpu.SemaphoreType.DMA((8,)),
            pltpu.SemaphoreType.DMA((34,)),
            pltpu.SemaphoreType.DMA((34,)),
        ],
        compiler_params=pltpu.CompilerParams(
            collective_id=0, has_side_effects=True, vmem_limit_bytes=56 << 20
        ),
        name="solidify",
    )(
        phases,
        node_temp,
        column_nodes.reshape(1, COLS),
        grain_ids.reshape(SLOT_ALL),
        grain_angle,
        grain_melt,
        heat_owner.reshape(POOL),
        heat_local,
    )
    return new.reshape(phases.shape), temp


def solution(mesh):
    placed = (
        P("ch", "tile", None, None),
        P("tile", None),
        P("tile"),
        P("tile", None),
        P(),
        P(),
        P("tile", None),
        P("tile"),
    )
    return jax.shard_map(
        on_device,
        mesh=mesh,
        in_specs=placed,
        out_specs=(P("ch", "tile", None, None), P("tile", None)),
        check_vma=False,
    )
```

time: 309 us -> 65.6 us (0.21)
  waiting for transfers between devices: 141 us -> 0 us
  starting transfers between devices: 118 us -> 0 us
  Pallas kernels: 0 us -> 62.2 us
  local copies, waits for them, and re-layouts: 18.6 us -> 2.56 us
  between operations: 14.5 us -> 0.65 us
  matrix products: 8.07 us -> 0 us
  other arithmetic: 7 us -> 0 us
    psum x2 -> x0, waiting for transfers between devices: 90.2 us -> none  [on_device(): heat = lax.psum(group_heat, 'ch')]
    ppermute x25 -> x0, starting transfers between devices: 66.2 us -> none  [the longest x21 55.2 us: shifted(): lax.ppermute(shard, axis, [(i, (i + by) % length) for i in range(length)])]
    pallas_call x0 -> x1, Pallas kernels: none -> 62.2 us  [on_device(): pl.pallas_call(kernel, out_shape=(jax.ShapeDtypeStruct((CH, COLS, NZ), F3...]
    all_to_all x3 -> x0, starting transfers between devices: 51.4 us -> none  [the longest x2 31 us: on_device(): lax.all_to_all(node_temp[wanted], 'tile', split_axis=0, concat_axis=0, ti...]
    all_to_all x3 -> x0, waiting for transfers between devices: 29.8 us -> none  [the longest x2 24.5 us: on_device(): lax.all_to_all(node_temp[wanted], 'tile', split_axis=0, concat_axis=0, ti...]
    ppermute x25 -> x0, waiting for transfers between devices: 19.9 us -> none  [the longest x21 18.2 us: shifted(): lax.ppermute(shard, axis, [(i, (i + by) % length) for i in range(length)])]
    scatter x4 -> x0, local copies, waits for them, and re-layouts: 10.3 us -> none  [the longest x1 6.37 us: on_device(): requests = jnp.zeros((tile_count, fetch_cap), jnp.int32).at[owners, fetch...]
    dot_general x6 -> x0, matrix products: 8.07 us -> none  [the longest x2 5.52 us: on_device(): jnp.einsum('ij,jxyz->ixyz', own_weights, everyone, preferred_element_type...]
  transfers between devices with their start and end apart: 32 -> 0, of which waited for: 13 -> 0; matrix products, arithmetic and copies ran while one was open for 4% -> 0% of each run, Pallas kernels for 0% -> 0%
where the time goes in v1:
time: 65.6 us; the launch traced here: 65.4 us
  Pallas kernels  62.2 us (95%)
  local copies, waits for them, and re-layouts  2.56 us (4%)
    pallas_call x1, Pallas kernels, on_device(): pl.pallas_call(kernel, out_shape=(jax.ShapeDtypeStruct((CH, COLS, NZ), F3...  62.2 us
    unnamed x4, local copies, waits for them, and re-layouts  2.56 us

profile of v1, /device:TPU:1, one launch (start us, length us, event | category | flops | bytes accessed | tf_op | source)
XLA Modules:
  0.0 65.4 jit_solution(5968696077343030844)
XLA Ops:
  0.6 62.2 %solidify.1 = (f32[8,128,128]{2,1,0:T(8,128)}, f32[256,128]{1,0:T(8,128)}) custom-call(f32[8,8,16,128]{3,2,1,0:T(8,128)} %phases_hbm.1, f32[256,128]{1,0:T(8,128)} %temp_hbm.1, s32[1,128]{1,0:T(1,128)} %bitcast.5, s32[32]{0:T(128)} %bitcast.6, f32[4096]{0:T(1024)} %angle_hbm.1, f32[4096]{0:T(1024)} %melt_hbm.1, s32[16]{0:T(128)} %bitcast.7, s32[16]{0:T(128)} %local_hbm.1), custom_call_target="tpu_custom_call" | custom-call | tf_op jit(solution)/shard_map/solidify/pallas_call | solution.py:574
  62.8 0.0 copy-start
  62.8 1.9 %copy.12 = f32[8,8,16,128]{3,2,1,0:T(8,128)} copy(f32[8,8,16,128]{3,2,1,0:T(8,128)} %bitcast.4) | data formatting | bytes 1048576
  64.7 0.0 copy-done
  64.8 0.7 %copy.13 = f32[256,128]{1,0:T(8,128)} copy(f32[256,128]{1,0:T(8,128)S(1)} %copy-done) | data formatting | bytes 262144
Async XLA Ops:
  62.8 1.9 %copy-start = (f32[256,128]{1,0:T(8,128)S(1)}, f32[256,128]{1,0:T(8,128)}, u32[]{:S(2)}) copy-start(f32[256,128]{1,0:T(8,128)} %get-tuple-element.9) | copy-start | bytes 393220

commit v2 on v1

--- a/solution.py
+++ b/solution.py
@@ -36,6 +36,7 @@
 FAR = BLOCK * SLOTS
 HEAT_ROWS = NEAR * HEAT_SLOTS
 HEAT_PAD = 32
+QUARTER = CH // 4
 
 
 def iota(shape, dim):
@@ -54,9 +55,12 @@
     return high, mid, low
 
 
-def pick(onehot, value):
-    high, mid, low = thirds(value)
-    return dot(onehot, high) + (dot(onehot, mid) + dot(onehot, low))
+def stacked(value):
+    return jnp.concatenate(thirds(value), axis=0)
+
+
+def tripled(onehot):
+    return jnp.concatenate([onehot, onehot, onehot], axis=1)
 
 
 def beside(values):
@@ -108,34 +112,42 @@
     partner = (group + GROUPS - block) % GROUPS
     inside = partner == block
 
+    first = partner * BLOCK
+    near_tiles = [lax.rem(tile + (TILES + step - REACH), TILES) for step in range(NEAR)]
+    groups = [group] + [lax.rem(group + turn, GROUPS) for turn in range(1, GROUPS)]
+    near_order = [
+        (offset, turn) for turn in (2, 1, 3, 0) for offset in (0, 6, 1, 5, 2, 4, 3)
+    ][:-1]
+
+    def far_index(number):
+        half = (number + 1) // 2
+        turn = jnp.where(number % 2 == 0, half, BLOCK - half)
+        return lax.rem(place + BLOCK // 2 + turn, BLOCK)
+
     def far_device(index):
-        return {"tile": partner * BLOCK + index, "ch": group}
+        return {"tile": first + index, "ch": group}
 
     def near_device(offset, turn):
-        return {"tile": (tile + offset + (TILES - REACH)) % TILES, "ch": (group + turn) % GROUPS}
+        return {"tile": near_tiles[offset], "ch": groups[turn]}
 
     barrier = pltpu.get_barrier_semaphore()
 
-    def greet_far(index, _):
-        @pl.when(jnp.logical_or(jnp.logical_not(inside), index != place))
-        def _():
-            pl.semaphore_signal(barrier, inc=1, device_id=far_device(index), device_id_type=MESH)
-
+    def greet_far(number, _):
+        pl.semaphore_signal(
+            barrier, inc=1, device_id=far_device(far_index(number)), device_id_type=MESH
+        )
         return 0
 
-    def greet_near(index, _):
-        offset, turn = index // GROUPS, index % GROUPS
-
-        @pl.when(jnp.logical_or(offset != REACH, turn != 0))
-        def _():
-            pl.semaphore_signal(
-                barrier, inc=1, device_id=near_device(offset, turn), device_id_type=MESH
-            )
-
-        return 0
-
-    lax.fori_loop(0, BLOCK, greet_far, 0)
-    lax.fori_loop(0, NEAR * GROUPS, greet_near, 0)
+    lax.fori_loop(0, BLOCK - 1, greet_far, 0)
+
+    @pl.when(jnp.logical_not(inside))
+    def _():
+        greet_far(BLOCK - 1, 0)
+
+    for offset, turn in near_order:
+        pl.semaphore_signal(
+            barrier, inc=1, device_id=near_device(offset, turn), device_id_type=MESH
+        )
 
     loads = [
         pltpu.make_async_copy(phases_hbm, cells.at[:, pl.ds(1, PX)], load_sem.at[0]),
@@ -172,10 +184,12 @@
     key_lane = iota((COLS, FAR), 1)
     take_own = jnp.where(key_lane + partner * FAR == key_down, 1.0, 0.0).astype(BF16)
     lane_all = iota((COLS, GROUPS * FAR), 1)
-    lane_block = (lane_all // FAR + GROUPS - block) % GROUPS
-    take_all = jnp.where(
+    lane_group = (group + GROUPS - lane_all // FAR) % GROUPS
+    lane_block = (lane_group + GROUPS - block) % GROUPS
+    take_turn = jnp.where(
         lane_block * FAR + lane_all % FAR == key_down, 1.0, 0.0
     ).astype(BF16)
+    take_own, take_turn = tripled(take_own), tripled(take_turn)
 
     row_down, lane = iota((POOL, COLS), 0), iota((POOL, COLS), 1)
     off_down = jnp.zeros((POOL, COLS), jnp.int32)
@@ -193,6 +207,7 @@
     pool_pick = jnp.where(spread, 1.0, 0.0).astype(BF16)
     row_of = jnp.where(iota((COLS, POOL), 0) == 8 * iota((COLS, POOL), 1), 1.0, 0.0).astype(BF16)
     row_pick = dot(pool_pick, row_of).astype(BF16)
+    pool_pick = tripled(pool_pick)
     flat[pl.ds(0, HEAT_PAD), :] = dot(row_pick, local_rows.astype(F32).astype(BF16))
     for offset in range(NEAR):
         target_out[offset] = flat[pl.ds(offset * HEAT_SLOTS, HEAT_SLOTS), :]
@@ -206,6 +221,9 @@
     total = (time_step * drive_gain) * total.reshape(COLS, NZ)
     own_v[0] = total
     all_v[0] = total
+
+    warm = conduct(temp[...])
+    cold_parts, warm_parts = stacked(temp[...]), stacked(warm)
 
     pl.semaphore_wait(
         barrier, NEAR * GROUPS - 1 + jnp.where(inside, BLOCK - 1, BLOCK).astype(jnp.int32)
@@ -222,14 +240,15 @@
         )
 
     def far_send(source, target, number):
-        def one(index, _):
-            @pl.when(jnp.logical_or(jnp.logical_not(inside), index != place))
-            def _():
-                far_copy(source, target, index, number).start()
-
+        def one(order, _):
+            far_copy(source, target, far_index(order), number).start()
             return 0
 
-        lax.fori_loop(0, BLOCK, one, 0)
+        lax.fori_loop(0, BLOCK - 1, one, 0)
+
+        @pl.when(jnp.logical_not(inside))
+        def _():
+            one(BLOCK - 1, 0)
 
         @pl.when(inside)
         def _():
@@ -246,23 +265,15 @@
             pltpu.make_async_copy(buffer, buffer, sem.at[number]).wait()
 
     def heat_send(source, target, number):
-        def one(index, _):
-            offset, turn = index // GROUPS, index % GROUPS
-
-            @pl.when(jnp.logical_or(offset != REACH, turn != 0))
-            def _():
-                pltpu.make_async_remote_copy(
-                    src_ref=source.at[offset],
-                    dst_ref=target.at[offset * GROUPS + group],
-                    send_sem=send_sem.at[number],
-                    recv_sem=recv_sem.at[number],
-                    device_id=near_device(offset, turn),
-                    device_id_type=MESH,
-                ).start()
-
-            return 0
-
-        lax.fori_loop(0, NEAR * GROUPS, one, 0)
+        for offset, turn in near_order:
+            pltpu.make_async_remote_copy(
+                src_ref=source.at[offset],
+                dst_ref=target.at[offset * GROUPS + group],
+                send_sem=send_sem.at[number],
+                recv_sem=recv_sem.at[number],
+                device_id=near_device(offset, turn),
+                device_id_type=MESH,
+            ).start()
         target[REACH * GROUPS + group] = source[REACH]
 
     def heat_done(buffer, sem, number):
@@ -270,21 +281,15 @@
         pltpu.make_async_copy(part, part, sem.at[number]).wait()
 
     def target_send(number):
-        def one(offset, _):
-            @pl.when(offset != REACH)
-            def _():
-                pltpu.make_async_remote_copy(
-                    src_ref=target_out.at[offset],
-                    dst_ref=target_in.at[offset],
-                    send_sem=send_sem.at[number],
-                    recv_sem=recv_sem.at[number],
-                    device_id=near_device(offset, 0),
-                    device_id_type=MESH,
-                ).start()
-
-            return 0
-
-        lax.fori_loop(0, NEAR, one, 0)
+        for offset in (0, 6, 1, 5, 2, 4):
+            pltpu.make_async_remote_copy(
+                src_ref=target_out.at[offset],
+                dst_ref=target_in.at[offset],
+                send_sem=send_sem.at[number],
+                recv_sem=recv_sem.at[number],
+                device_id=near_device(offset, 0),
+                device_id_type=MESH,
+            ).start()
         target_in[REACH] = target_out[REACH]
 
     def target_done(buffer, sem, number):
@@ -303,6 +308,27 @@
             )
             for turn in range(1, GROUPS)
         ]
+
+    def ring_copies(buffer, number):
+        def move(owner, part, turn, order):
+            piece = buffer.at[owner, pl.ds(part * QUARTER, QUARTER)]
+            return pltpu.make_async_remote_copy(
+                src_ref=piece,
+                dst_ref=piece,
+                send_sem=send_sem.at[number + order],
+                recv_sem=recv_sem.at[number + order],
+                device_id=near_device(REACH, turn),
+                device_id_type=MESH,
+            )
+
+        right = [move(group, part, 1, part) for part in (0, 1, 2, 3)]
+        left = [move(group, part, 3, 4 + part) for part in (2, 3, 0, 1)]
+        starts = [copy for pair in zip(right, left) for copy in pair]
+        onward = []
+        for step in range(2):
+            onward.append(move(groups[3], step, 1, 8 + step))
+            onward.append(move(groups[1], step + 2, 3, 10 + step))
+        return starts, starts[:4], onward, starts[4:] + onward
 
     def halo_copies(buffer, number):
         return [
@@ -326,7 +352,7 @@
 
     REQ, ROWS, ROWS2, HEAT, HEAT2, TARGET = 0, 1, 2, 3, 4, 5
     HALO, HALO2 = 6, 8
-    GATHER, GATHER2, SHARE, SHARE2, VEE, VEE2 = 10, 14, 18, 22, 26, 30
+    GATHER, GATHER2, SHARE, SHARE2, VEE, VEE2 = 10, 14, 26, 30, 34, 38
 
     far_send(req_out, req_in, REQ)
     target_send(TARGET)
@@ -410,7 +436,8 @@
         for index in range(BLOCK):
             kept[0, pl.ds(index * SLOTS, SLOTS), :] = buffer[index]
 
-    spread_rows(pick(serve, temp[...]), rows_out)
+    serve = tripled(serve)
+    spread_rows(dot(serve, cold_parts), rows_out)
     far_send(rows_out, rows_in, ROWS)
 
     target_done(target_in, recv_sem, TARGET)
@@ -422,9 +449,9 @@
     low = jnp.where(aims == iota((NZ, NZ), 1), 1.0, 0.0).T
     high = jnp.where(aims == iota((NZ, NZ), 1) + NZ, 1.0, 0.0).T
     scatter = jnp.concatenate([low, high], axis=0)[:, :HEAT_PAD].astype(BF16)
-    relay = dot(serve, scatter).astype(BF16)
-    warm = conduct(temp[...])
-    warm_rows = pick(serve, warm)
+    relay = tripled(dot(serve[:, :NODES], scatter).astype(BF16))
+    scatter = tripled(scatter)
+    warm_rows = dot(serve, warm_parts)
     heat_flat[...] = jnp.zeros((HEAT_PAD, NZ), F32)
 
     def arrived_heat(buffer):
@@ -436,26 +463,15 @@
         return heat_flat[...]
 
     def send_heat(kept, own_part, vee, out, target, number):
-        mine = pick(take_own, kept[0])
+        mine = dot(take_own, stacked(kept[0]))
         amount = own_part - mine * vee
-        flat[pl.ds(0, HEAT_PAD), :] = pick(pool_pick, amount)
+        flat[pl.ds(0, HEAT_PAD), :] = dot(pool_pick, stacked(amount))
         for offset in range(NEAR):
             out[offset] = flat[pl.ds(offset * HEAT_SLOTS, HEAT_SLOTS), :]
         heat_send(out, target, number)
 
     def share_copies(buffer, number):
         return group_copies(lambda turn: buffer.at[0], lambda turn: buffer.at[turn], number)
-
-    turn_of = (group + GROUPS - lane_all // FAR) % GROUPS
-    del turn_of
-    take_turn = jnp.where(
-        (((group + GROUPS - lane_all // FAR) % GROUPS + GROUPS - block) % GROUPS) * FAR
-        + lane_all % FAR
-        == key_down,
-        1.0,
-        0.0,
-    ).astype(BF16)
-    del take_all
 
     for copy in vees:
         copy.wait_recv()
@@ -467,7 +483,6 @@
     shares = share_copies(share, SHARE)
     for copy in shares:
         copy.start()
-
     for copy in gathers:
         copy.wait_recv()
     mix(gathered)
@@ -475,7 +490,7 @@
         copy.wait_recv()
 
     def all_rows(kept):
-        return pick(take_turn, kept[...].reshape(GROUPS * FAR, NZ))
+        return dot(take_turn, stacked(kept[...].reshape(GROUPS * FAR, NZ)))
 
     cell_temp = all_rows(share)
 
@@ -495,20 +510,21 @@
     all_v2[0] = total
     halos2 = halo_copies(cells2, HALO2)
     vees2 = group_copies(lambda turn: own_v.at[1], lambda turn: all_v2.at[turn], VEE2)
-    gathers2 = group_copies(
-        lambda turn: gathered2.at[group], lambda turn: gathered2.at[group], GATHER2
-    )
-    for copy in halos2 + vees2 + gathers2:
+    ring2 = ring_copies(gathered2, GATHER2)
+    for copy in vees2 + halos2 + ring2[0]:
         copy.start()
 
     heat_done(heat_in, recv_sem, HEAT)
     arrived = arrived_heat(heat_in)
-    spread_rows(warm_rows + heat_gain * pick(relay, arrived), rows_out2)
+    spread_rows(warm_rows + heat_gain * dot(relay, stacked(arrived)), rows_out2)
     far_send(rows_out2, rows_in2, ROWS2)
-    final_temp[...] = conduct(warm + heat_gain * pick(scatter, arrived))
+    final_temp[...] = conduct(warm + heat_gain * dot(scatter, stacked(arrived)))
 
     for copy in halos2:
         copy.wait_recv()
+    for arrived_copy, onward in zip(ring2[1], ring2[2]):
+        arrived_copy.wait_recv()
+        onward.start()
     own_u2 = stencil(cells2, static2)
     for copy in vees2:
         copy.wait_recv()
@@ -521,7 +537,7 @@
     for copy in shares2:
         copy.start()
 
-    for copy in gathers2:
+    for copy in ring2[3]:
         copy.wait_recv()
     mix(gathered2)
     for copy in shares2:
@@ -532,8 +548,7 @@
         now = cells2[channel, pl.ds(1, PX)].reshape(COLS, NZ)
         change = (time_step * drive_gain) * cell_temp2 * (now - now * now)
         mixing = mixed[channel].reshape(COLS, NZ)
-        new = static2[channel] - time_step * mixing - change
-        static2[channel] = new
+        static2[channel] = static2[channel] - time_step * mixing - change
         return 0
 
     lax.fori_loop(0, CH, finish, 0)
@@ -542,7 +557,7 @@
 
     heat_done(heat_in2, recv_sem, HEAT2)
     arrived = arrived_heat(heat_in2)
-    final_temp[...] = final_temp[...] + heat_gain * pick(scatter, arrived)
+    final_temp[...] = final_temp[...] + heat_gain * dot(scatter, stacked(arrived))
     store_temp = pltpu.make_async_copy(final_temp, temp_out, load_sem.at[1])
     store_temp.start()
 
@@ -552,20 +567,42 @@
     heat_done(heat_in, send_sem, HEAT)
     heat_done(heat_in2, send_sem, HEAT2)
     target_done(target_out, send_sem, TARGET)
-    for copy in halos + vees + gathers + shares + halos2 + vees2 + gathers2 + shares2:
+    for copy in halos + vees + gathers + shares + halos2 + vees2 + ring2[0] + ring2[2] + shares2:
         copy.wait_send()
     store.wait()
     store_temp.wait()
 
 
+def place_results(new, temp, new_out, temp_out, new_held, temp_held, load_sem, store_sem):
+    moves = [(temp, temp_held, temp_out)] + [
+        (new.at[channel], new_held.at[channel], new_out.at[channel]) for channel in range(CH)
+    ]
+    loads = [
+        pltpu.make_async_copy(source, held, load_sem.at[number])
+        for number, (source, held, _) in enumerate(moves)
+    ]
+    stores = [
+        pltpu.make_async_copy(held, target, store_sem.at[number])
+        for number, (_, held, target) in enumerate(moves)
+    ]
+    for load in loads:
+        load.start()
+    for load, store in zip(loads, stores):
+        load.wait()
+        store.start()
+    for store in stores:
+        store.wait()
+
+
 def on_device(
     phases, node_temp, column_nodes, grain_ids, grain_angle, grain_melt, heat_owner, heat_local
 ):
-    anywhere = pl.BlockSpec(memory_space=pl.ANY)
+    outside = pl.BlockSpec(memory_space=pl.ANY)
     vmem, smem = pltpu.VMEM, pltpu.SMEM
     gathered = vmem((GROUPS, CH, PX, PY, NZ), BF16)
     padded = vmem((CH, PX + 2, PY, NZ), F32)
     flat_cells = vmem((CH, COLS, NZ), F32)
+    mix_out = vmem((CH, PX, PY, NZ), F32)
     far_rows = vmem((BLOCK, SLOTS, NZ), F32)
     shared = vmem((GROUPS, FAR, NZ), F32)
     heat_out = vmem((NEAR, HEAT_SLOTS, NZ), F32)
@@ -577,10 +614,10 @@
             jax.ShapeDtypeStruct((CH, COLS, NZ), F32),
             jax.ShapeDtypeStruct(node_temp.shape, F32),
         ),
-        in_specs=[anywhere] * 8,
-        out_specs=(anywhere, anywhere),
+        in_specs=[outside] * 8,
+        out_specs=(outside, outside),
         scratch_shapes=[
-            padded, padded, flat_cells, flat_cells, vmem((CH, PX, PY, NZ), F32), gathered, gathered,
+            padded, padded, flat_cells, flat_cells, mix_out, gathered, gathered,
             vmem((NODES, NZ), F32), vmem((1, COLS), jnp.int32), smem((SLOT_ALL,), jnp.int32),
             smem((grain_angle.shape[0],), F32), smem((grain_melt.shape[0],), F32),
             smem((POOL,), jnp.int32), smem((POOL,), jnp.int32),
@@ -589,8 +626,8 @@
             vmem((2, COLS, NZ), F32), field, field, vmem((FAR, NZ), F32), vmem((HEAT_PAD, NZ), F32),
             vmem((NODES, NZ), F32),
             pltpu.SemaphoreType.DMA((8,)),
-            pltpu.SemaphoreType.DMA((34,)),
-            pltpu.SemaphoreType.DMA((34,)),
+            pltpu.SemaphoreType.DMA((42,)),
+            pltpu.SemaphoreType.DMA((42,)),
         ],
         compiler_params=pltpu.CompilerParams(
             collective_id=0, has_side_effects=True, vmem_limit_bytes=56 << 20
@@ -606,7 +643,23 @@
         heat_owner.reshape(POOL),
         heat_local,
     )
-    return new.reshape(phases.shape), temp
+    placed, temp = pl.pallas_call(
+        place_results,
+        out_shape=(
+            jax.ShapeDtypeStruct(new.shape, F32),
+            jax.ShapeDtypeStruct(temp.shape, F32),
+        ),
+        in_specs=[outside] * 2,
+        out_specs=(outside, outside),
+        scratch_shapes=[
+            vmem(new.shape, F32),
+            vmem(temp.shape, F32),
+            pltpu.SemaphoreType.DMA((CH + 1,)),
+            pltpu.SemaphoreType.DMA((CH + 1,)),
+        ],
+        name="results",
+    )(new, temp)
+    return placed.reshape(phases.shape), temp
 
 
 def solution(mesh):

time: 65.6 us -> 60.1 us (0.916)
  Pallas kernels: 62.2 us -> 59.3 us
  local copies, waits for them, and re-layouts: 2.56 us -> 0 us
    pallas_call x1, Pallas kernels: 62.2 us -> 57.4 us  [on_device(): pl.pallas_call(kernel, out_shape=(jax.ShapeDtypeStruct((CH, COLS, NZ), F3...]
    unnamed x4 -> x0, local copies, waits for them, and re-layouts: 2.56 us -> none
    pallas_call x0 -> x1, Pallas kernels: none -> 1.9 us  [on_device(): pl.pallas_call(place_results, out_shape=(jax.ShapeDtypeStruct(new.shape,...]
where the time goes in v2:
time: 60.1 us; the launch traced here: 59.9 us
  Pallas kernels  59.3 us (99%)
  between operations  0.64 us (1%)
    pallas_call x1, Pallas kernels, on_device(): pl.pallas_call(kernel, out_shape=(jax.ShapeDtypeStruct((CH, COLS, NZ), F3...  57.4 us
    pallas_call x1, Pallas kernels, on_device(): pl.pallas_call(place_results, out_shape=(jax.ShapeDtypeStruct(new.shape,...  1.9 us

profile of v2, /device:TPU:1, one launch (start us, length us, event | category | flops | bytes accessed | tf_op | source)
XLA Modules:
  0.0 59.9 jit_solution(2202956078080132997)
XLA Ops:
  0.6 57.4 %solidify.1 = (f32[8,128,128]{2,1,0:T(8,128)}, f32[256,128]{1,0:T(8,128)}) custom-call(f32[8,8,16,128]{3,2,1,0:T(8,128)} %phases_hbm.1, f32[256,128]{1,0:T(8,128)} %temp_hbm.1, s32[1,128]{1,0:T(1,128)} %bitcast.4, s32[32]{0:T(128)} %bitcast.5, f32[4096]{0:T(1024)} %angle_hbm.1, f32[4096]{0:T(1024)} %melt_hbm.1, s32[16]{0:T(128)} %bitcast.6, s32[16]{0:T(128)} %local_hbm.1), custom_call_target="tpu_custom_call" | custom-call | tf_op jit(solution)/shard_map/solidify/pallas_call | solution.py:611
  58.0 1.9 %results.1 = (f32[8,128,128]{2,1,0:T(8,128)}, f32[256,128]{1,0:T(8,128)}) custom-call(f32[8,128,128]{2,1,0:T(8,128)} %get-tuple-element.6.new, f32[256,128]{1,0:T(8,128)} %get-tuple-element.7.temp), custom_call_target="tpu_custom_call" | custom-call | tf_op jit(solution)/shard_map/results/pallas_call | solution.py:646

commit v3 on v2

--- a/solution.py
+++ b/solution.py
@@ -102,7 +102,7 @@
     temp, columns, grains, angles, melts, owners, locals_,
     req_out, req_in, rows_out, rows_in, rows_out2, rows_in2, share, share2,
     heat_out, heat_in, heat_out2, heat_in2, target_out, target_in,
-    own_v, all_v, all_v2, flat, heat_flat, final_temp,
+    own_v, own_v2, all_v, all_v2, by_owner, flat, heat_flat, final_temp,
     load_sem, send_sem, recv_sem,
 ):
     tile = lax.axis_index("tile")
@@ -183,13 +183,17 @@
         req_out[index] = flat[pl.ds(index * SLOTS, SLOTS), :]
     key_lane = iota((COLS, FAR), 1)
     take_own = jnp.where(key_lane + partner * FAR == key_down, 1.0, 0.0).astype(BF16)
+    row_all = iota((GROUPS * FAR, COLS), 0)
+    row_block = ((group + row_all // FAR) % GROUPS + GROUPS - block) % GROUPS
+    give_all = jnp.where(row_block * FAR + row_all % FAR == key_over, 1.0, 0.0).astype(BF16)
+    give_all = tripled(give_all)
     lane_all = iota((COLS, GROUPS * FAR), 1)
     lane_group = (group + GROUPS - lane_all // FAR) % GROUPS
     lane_block = (lane_group + GROUPS - block) % GROUPS
     take_turn = jnp.where(
         lane_block * FAR + lane_all % FAR == key_down, 1.0, 0.0
     ).astype(BF16)
-    take_own, take_turn = tripled(take_own), tripled(take_turn)
+    take_turn = tripled(take_turn)
 
     row_down, lane = iota((POOL, COLS), 0), iota((POOL, COLS), 1)
     off_down = jnp.zeros((POOL, COLS), jnp.int32)
@@ -207,6 +211,7 @@
     pool_pick = jnp.where(spread, 1.0, 0.0).astype(BF16)
     row_of = jnp.where(iota((COLS, POOL), 0) == 8 * iota((COLS, POOL), 1), 1.0, 0.0).astype(BF16)
     row_pick = dot(pool_pick, row_of).astype(BF16)
+    slot_pick = tripled(dot(pool_pick, take_own).astype(BF16))
     pool_pick = tripled(pool_pick)
     flat[pl.ds(0, HEAT_PAD), :] = dot(row_pick, local_rows.astype(F32).astype(BF16))
     for offset in range(NEAR):
@@ -219,8 +224,7 @@
 
     total = lax.fori_loop(0, CH, first_look, jnp.zeros((PX, PY, NZ), F32))
     total = (time_step * drive_gain) * total.reshape(COLS, NZ)
-    own_v[0] = total
-    all_v[0] = total
+    own_v[...] = dot(give_all, stacked(total)).reshape(GROUPS, FAR, NZ)
 
     warm = conduct(temp[...])
     cold_parts, warm_parts = stacked(temp[...]), stacked(warm)
@@ -357,7 +361,7 @@
     far_send(req_out, req_in, REQ)
     target_send(TARGET)
     halos = halo_copies(cells, HALO)
-    vees = group_copies(lambda turn: own_v.at[0], lambda turn: all_v.at[turn], VEE)
+    vees = group_copies(lambda turn: own_v.at[turn], lambda turn: all_v.at[turn], VEE)
     gathers = group_copies(
         lambda turn: gathered.at[group], lambda turn: gathered.at[group], GATHER
     )
@@ -383,6 +387,8 @@
     weights = dot(tall, widen)
     weights = jnp.where(iota(wide_shape, 0) % PY == iota(wide_shape, 1) % PY, weights, 0.0)
     weights = weights.astype(BF16)
+    for owner in range(GROUPS):
+        by_owner[owner] = weights[:, owner * COLS : (owner + 1) * COLS]
 
     def melt_of(channel):
         return melts[grains[group * CH + channel]]
@@ -463,9 +469,8 @@
         return heat_flat[...]
 
     def send_heat(kept, own_part, vee, out, target, number):
-        mine = dot(take_own, stacked(kept[0]))
-        amount = own_part - mine * vee
-        flat[pl.ds(0, HEAT_PAD), :] = dot(pool_pick, stacked(amount))
+        warmed = dot(slot_pick, stacked(kept[0] * vee))
+        flat[pl.ds(0, HEAT_PAD), :] = own_part - warmed
         for offset in range(NEAR):
             out[offset] = flat[pl.ds(offset * HEAT_SLOTS, HEAT_SLOTS), :]
         heat_send(out, target, number)
@@ -475,11 +480,12 @@
 
     for copy in vees:
         copy.wait_recv()
-    vee = (all_v[0] + all_v[1]) + (all_v[2] + all_v[3])
+    vee = (own_v[0] + all_v[1]) + (all_v[2] + all_v[3])
+    fixed_heat = dot(pool_pick, stacked(own_u))
 
     far_done(rows_in, recv_sem, ROWS)
     collect_rows(rows_in, share)
-    send_heat(share, own_u, vee, heat_out, heat_in, HEAT)
+    send_heat(share, fixed_heat, vee, heat_out, heat_in, HEAT)
     shares = share_copies(share, SHARE)
     for copy in shares:
         copy.start()
@@ -506,10 +512,9 @@
 
     total = lax.fori_loop(0, CH, update, jnp.zeros((COLS, NZ), F32))
     total = (time_step * drive_gain) * total
-    own_v[1] = total
-    all_v2[0] = total
+    own_v2[...] = dot(give_all, stacked(total)).reshape(GROUPS, FAR, NZ)
     halos2 = halo_copies(cells2, HALO2)
-    vees2 = group_copies(lambda turn: own_v.at[1], lambda turn: all_v2.at[turn], VEE2)
+    vees2 = group_copies(lambda turn: own_v2.at[turn], lambda turn: all_v2.at[turn], VEE2)
     ring2 = ring_copies(gathered2, GATHER2)
     for copy in vees2 + halos2 + ring2[0]:
         copy.start()
@@ -528,18 +533,31 @@
     own_u2 = stencil(cells2, static2)
     for copy in vees2:
         copy.wait_recv()
-    vee2 = (all_v2[0] + all_v2[1]) + (all_v2[2] + all_v2[3])
+    vee2 = (own_v2[0] + all_v2[1]) + (all_v2[2] + all_v2[3])
+    fixed_heat2 = dot(pool_pick, stacked(own_u2))
 
     far_done(rows_in2, recv_sem, ROWS2)
     collect_rows(rows_in2, share2)
-    send_heat(share2, own_u2, vee2, heat_out2, heat_in2, HEAT2)
+    send_heat(share2, fixed_heat2, vee2, heat_out2, heat_in2, HEAT2)
     shares2 = share_copies(share2, SHARE2)
     for copy in shares2:
         copy.start()
 
-    for copy in ring2[3]:
-        copy.wait_recv()
-    mix(gathered2)
+    for copy in ring2[3][:4]:
+        copy.wait_recv()
+
+    def block_of(owner, plane):
+        right = gathered2[owner, :, plane].reshape(COLS, NZ)
+        return dot(by_owner[owner], right).reshape(CH, PY, NZ)
+
+    for plane in range(PX):
+        mixed[:, plane] = block_of(group, plane) + (
+            block_of(groups[1], plane) + block_of(groups[3], plane)
+        )
+    for copy in ring2[3][4:]:
+        copy.wait_recv()
+    for plane in range(PX):
+        mixed[:, plane] += block_of(groups[2], plane)
     for copy in shares2:
         copy.wait_recv()
     cell_temp2 = all_rows(share2)
@@ -607,7 +625,6 @@
     shared = vmem((GROUPS, FAR, NZ), F32)
     heat_out = vmem((NEAR, HEAT_SLOTS, NZ), F32)
     heat_in = vmem((NEAR * GROUPS, HEAT_SLOTS, NZ), F32)
-    field = vmem((GROUPS, COLS, NZ), F32)
     new, temp = pl.pallas_call(
         kernel,
         out_shape=(
@@ -623,7 +640,7 @@
             smem((POOL,), jnp.int32), smem((POOL,), jnp.int32),
             far_rows, far_rows, far_rows, far_rows, far_rows, far_rows, shared, shared,
             heat_out, heat_in, heat_out, heat_in, heat_out, heat_out,
-            vmem((2, COLS, NZ), F32), field, field, vmem((FAR, NZ), F32), vmem((HEAT_PAD, NZ), F32),
+            shared, shared, shared, shared, vmem((GROUPS, COLS, COLS), BF16), vmem((FAR, NZ), F32), vmem((HEAT_PAD, NZ), F32),
             vmem((NODES, NZ), F32),
             pltpu.SemaphoreType.DMA((8,)),
             pltpu.SemaphoreType.DMA((42,)),

time: 60.1 us -> 59 us (0.982)
  Pallas kernels: 59.3 us -> 58.2 us
    pallas_call x1, Pallas kernels: 57.4 us -> 56.3 us  [on_device(): pl.pallas_call(kernel, out_shape=(jax.ShapeDtypeStruct((CH, COLS, NZ), F3...]
where the time goes in v3:
time: 59 us; the launch traced here: 58.8 us
  Pallas kernels  58.2 us (99%)
  between operations  0.64 us (1%)
    pallas_call x1, Pallas kernels, on_device(): pl.pallas_call(kernel, out_shape=(jax.ShapeDtypeStruct((CH, COLS, NZ), F3...  56.3 us
    pallas_call x1, Pallas kernels, on_device(): pl.pallas_call(place_results, out_shape=(jax.ShapeDtypeStruct(new.shape,...  1.9 us

profile of v3, /device:TPU:1, one launch (start us, length us, event | category | flops | bytes accessed | tf_op | source)
XLA Modules:
  0.0 58.8 jit_solution(3069299584137350706)
XLA Ops:
  0.6 56.3 %solidify.1 = (f32[8,128,128]{2,1,0:T(8,128)}, f32[256,128]{1,0:T(8,128)}) custom-call(f32[8,8,16,128]{3,2,1,0:T(8,128)} %phases_hbm.1, f32[256,128]{1,0:T(8,128)} %temp_hbm.1, s32[1,128]{1,0:T(1,128)} %bitcast.4, s32[32]{0:T(128)} %bitcast.5, f32[4096]{0:T(1024)} %angle_hbm.1, f32[4096]{0:T(1024)} %melt_hbm.1, s32[16]{0:T(128)} %bitcast.6, s32[16]{0:T(128)} %local_hbm.1), custom_call_target="tpu_custom_call" | custom-call | tf_op jit(solution)/shard_map/solidify/pallas_call | solution.py:628
  56.9 1.9 %results.1 = (f32[8,128,128]{2,1,0:T(8,128)}, f32[256,128]{1,0:T(8,128)}) custom-call(f32[8,128,128]{2,1,0:T(8,128)} %get-tuple-element.6.new, f32[256,128]{1,0:T(8,128)} %get-tuple-element.7.temp), custom_call_target="tpu_custom_call" | custom-call | tf_op jit(solution)/shard_map/results/pallas_call | solution.py:663

commit v4 on v3

--- a/solution.py
+++ b/solution.py
@@ -485,10 +485,10 @@
 
     far_done(rows_in, recv_sem, ROWS)
     collect_rows(rows_in, share)
-    send_heat(share, fixed_heat, vee, heat_out, heat_in, HEAT)
     shares = share_copies(share, SHARE)
     for copy in shares:
         copy.start()
+    send_heat(share, fixed_heat, vee, heat_out, heat_in, HEAT)
     for copy in gathers:
         copy.wait_recv()
     mix(gathered)
@@ -511,12 +511,14 @@
         return total + (new - new * new)
 
     total = lax.fori_loop(0, CH, update, jnp.zeros((COLS, NZ), F32))
+    ring2 = ring_copies(gathered2, GATHER2)
+    for copy in ring2[0][:4]:
+        copy.start()
     total = (time_step * drive_gain) * total
     own_v2[...] = dot(give_all, stacked(total)).reshape(GROUPS, FAR, NZ)
     halos2 = halo_copies(cells2, HALO2)
     vees2 = group_copies(lambda turn: own_v2.at[turn], lambda turn: all_v2.at[turn], VEE2)
-    ring2 = ring_copies(gathered2, GATHER2)
-    for copy in vees2 + halos2 + ring2[0]:
+    for copy in vees2 + halos2 + ring2[0][4:]:
         copy.start()
 
     heat_done(heat_in, recv_sem, HEAT)
@@ -562,21 +564,22 @@
         copy.wait_recv()
     cell_temp2 = all_rows(share2)
 
-    def finish(channel, _):
+    stores = []
+    for channel in range(CH):
         now = cells2[channel, pl.ds(1, PX)].reshape(COLS, NZ)
         change = (time_step * drive_gain) * cell_temp2 * (now - now * now)
         mixing = mixed[channel].reshape(COLS, NZ)
         static2[channel] = static2[channel] - time_step * mixing - change
-        return 0
-
-    lax.fori_loop(0, CH, finish, 0)
-    store = pltpu.make_async_copy(static2, phases_out, load_sem.at[0])
-    store.start()
+        store = pltpu.make_async_copy(
+            static2.at[channel], phases_out.at[channel], load_sem.at[channel]
+        )
+        store.start()
+        stores.append(store)
 
     heat_done(heat_in2, recv_sem, HEAT2)
     arrived = arrived_heat(heat_in2)
     final_temp[...] = final_temp[...] + heat_gain * dot(scatter, stacked(arrived))
-    store_temp = pltpu.make_async_copy(final_temp, temp_out, load_sem.at[1])
+    store_temp = pltpu.make_async_copy(final_temp, temp_out, load_sem.at[CH])
     store_temp.start()
 
     far_done(req_out, send_sem, REQ)
@@ -587,29 +590,13 @@
     target_done(target_out, send_sem, TARGET)
     for copy in halos + vees + gathers + shares + halos2 + vees2 + ring2[0] + ring2[2] + shares2:
         copy.wait_send()
-    store.wait()
-    store_temp.wait()
-
-
-def place_results(new, temp, new_out, temp_out, new_held, temp_held, load_sem, store_sem):
-    moves = [(temp, temp_held, temp_out)] + [
-        (new.at[channel], new_held.at[channel], new_out.at[channel]) for channel in range(CH)
-    ]
-    loads = [
-        pltpu.make_async_copy(source, held, load_sem.at[number])
-        for number, (source, held, _) in enumerate(moves)
-    ]
-    stores = [
-        pltpu.make_async_copy(held, target, store_sem.at[number])
-        for number, (_, held, target) in enumerate(moves)
-    ]
-    for load in loads:
-        load.start()
-    for load, store in zip(loads, stores):
-        load.wait()
-        store.start()
-    for store in stores:
+    for store in stores + [store_temp]:
         store.wait()
+
+
+def place_results(new, temp, new_out, temp_out):
+    new_out[...] = new[...]
+    temp_out[...] = temp[...]
 
 
 def on_device(
@@ -642,7 +629,7 @@
             heat_out, heat_in, heat_out, heat_in, heat_out, heat_out,
             shared, shared, shared, shared, vmem((GROUPS, COLS, COLS), BF16), vmem((FAR, NZ), F32), vmem((HEAT_PAD, NZ), F32),
             vmem((NODES, NZ), F32),
-            pltpu.SemaphoreType.DMA((8,)),
+            pltpu.SemaphoreType.DMA((CH + 1,)),
             pltpu.SemaphoreType.DMA((42,)),
             pltpu.SemaphoreType.DMA((42,)),
         ],
@@ -660,20 +647,19 @@
         heat_owner.reshape(POOL),
         heat_local,
     )
+    halves = (
+        pl.BlockSpec((CH // 2, COLS, NZ), lambda half: (half, 0, 0)),
+        pl.BlockSpec((NODES // 2, NZ), lambda half: (half, 0)),
+    )
     placed, temp = pl.pallas_call(
         place_results,
         out_shape=(
             jax.ShapeDtypeStruct(new.shape, F32),
             jax.ShapeDtypeStruct(temp.shape, F32),
         ),
-        in_specs=[outside] * 2,
-        out_specs=(outside, outside),
-        scratch_shapes=[
-            vmem(new.shape, F32),
-            vmem(temp.shape, F32),
-            pltpu.SemaphoreType.DMA((CH + 1,)),
-            pltpu.SemaphoreType.DMA((CH + 1,)),
-        ],
+        grid=(2,),
+        in_specs=halves,
+        out_specs=halves,
         name="results",
     )(new, temp)
     return placed.reshape(phases.shape), temp

time: 59 us -> 58.4 us (0.990)
  Pallas kernels: 58.2 us -> 57.6 us
where the time goes in v4:
time: 58.4 us; the launch traced here: 58.2 us
  Pallas kernels  57.6 us (99%)
  between operations  0.64 us (1%)
    pallas_call x1, Pallas kernels, on_device(): pl.pallas_call(kernel, out_shape=(jax.ShapeDtypeStruct((CH, COLS, NZ), F3...  55.8 us
    pallas_call x1, Pallas kernels, on_device(): pl.pallas_call(place_results, out_shape=(jax.ShapeDtypeStruct(new.shape,...  1.82 us

profile of v4, /device:TPU:1, one launch (start us, length us, event | category | flops | bytes accessed | tf_op | source)
XLA Modules:
  0.0 58.2 jit_solution(16493727426159224064)
XLA Ops:
  0.6 55.8 %solidify.1 = (f32[8,128,128]{2,1,0:T(8,128)}, f32[256,128]{1,0:T(8,128)}) custom-call(f32[8,8,16,128]{3,2,1,0:T(8,128)} %phases_hbm.1, f32[256,128]{1,0:T(8,128)} %temp_hbm.1, s32[1,128]{1,0:T(1,128)} %bitcast.4, s32[32]{0:T(128)} %bitcast.5, f32[4096]{0:T(1024)} %angle_hbm.1, f32[4096]{0:T(1024)} %melt_hbm.1, s32[16]{0:T(128)} %bitcast.6, s32[16]{0:T(128)} %local_hbm.1), custom_call_target="tpu_custom_call" | custom-call | tf_op jit(solution)/shard_map/solidify/pallas_call | solution.py:615
  56.4 1.8 %results.1 = (f32[8,128,128]{2,1,0:T(8,128)}, f32[256,128]{1,0:T(8,128)}) custom-call(f32[8,128,128]{2,1,0:T(8,128)} %get-tuple-element.6.new, f32[256,128]{1,0:T(8,128)} %get-tuple-element.7.temp), custom_call_target="tpu_custom_call" | custom-call | tf_op jit(solution)/shard_map/results/pallas_call | solution.py:654

commit v5 on v4

--- a/solution.py
+++ b/solution.py
@@ -161,8 +161,7 @@
     ]
     for load in loads:
         load.start()
-    for load in loads:
-        load.wait()
+    loads[2].wait()
 
     wanted = jnp.broadcast_to(columns[...].astype(F32), (COLS, COLS))
     wanted_down = wanted.T
@@ -181,6 +180,140 @@
     flat[pl.ds(0, FAR), :] = dot(ask, local_down.astype(BF16))
     for index in range(BLOCK):
         req_out[index] = flat[pl.ds(index * SLOTS, SLOTS), :]
+    pl.semaphore_wait(
+        barrier, NEAR * GROUPS - 1 + jnp.where(inside, BLOCK - 1, BLOCK).astype(jnp.int32)
+    )
+
+    def far_copy(source, target, index, number):
+        return pltpu.make_async_remote_copy(
+            src_ref=source.at[index],
+            dst_ref=target.at[place],
+            send_sem=send_sem.at[number],
+            recv_sem=recv_sem.at[number],
+            device_id=far_device(index),
+            device_id_type=MESH,
+        )
+
+    def far_send(source, target, number):
+        def one(order, _):
+            far_copy(source, target, far_index(order), number).start()
+            return 0
+
+        lax.fori_loop(0, BLOCK - 1, one, 0)
+
+        @pl.when(jnp.logical_not(inside))
+        def _():
+            one(BLOCK - 1, 0)
+
+        @pl.when(inside)
+        def _():
+            target[place] = source[place]
+
+    def far_done(buffer, sem, number):
+        @pl.when(inside)
+        def _():
+            part = buffer.at[pl.ds(0, BLOCK - 1)]
+            pltpu.make_async_copy(part, part, sem.at[number]).wait()
+
+        @pl.when(jnp.logical_not(inside))
+        def _():
+            pltpu.make_async_copy(buffer, buffer, sem.at[number]).wait()
+
+    def heat_send(source, target, number):
+        for offset, turn in near_order:
+            pltpu.make_async_remote_copy(
+                src_ref=source.at[offset],
+                dst_ref=target.at[offset * GROUPS + group],
+                send_sem=send_sem.at[number],
+                recv_sem=recv_sem.at[number],
+                device_id=near_device(offset, turn),
+                device_id_type=MESH,
+            ).start()
+        target[REACH * GROUPS + group] = source[REACH]
+
+    def heat_done(buffer, sem, number):
+        part = buffer.at[pl.ds(0, NEAR * GROUPS - 1)]
+        pltpu.make_async_copy(part, part, sem.at[number]).wait()
+
+    def target_send(number):
+        for offset in (0, 6, 1, 5, 2, 4):
+            pltpu.make_async_remote_copy(
+                src_ref=target_out.at[offset],
+                dst_ref=target_in.at[offset],
+                send_sem=send_sem.at[number],
+                recv_sem=recv_sem.at[number],
+                device_id=near_device(offset, 0),
+                device_id_type=MESH,
+            ).start()
+        target_in[REACH] = target_out[REACH]
+
+    def target_done(buffer, sem, number):
+        part = buffer.at[pl.ds(0, NEAR - 1)]
+        pltpu.make_async_copy(part, part, sem.at[number]).wait()
+
+    def group_copies(source_of, target_of, number):
+        return [
+            pltpu.make_async_remote_copy(
+                src_ref=source_of(turn),
+                dst_ref=target_of(turn),
+                send_sem=send_sem.at[number + turn],
+                recv_sem=recv_sem.at[number + turn],
+                device_id=near_device(REACH, turn),
+                device_id_type=MESH,
+            )
+            for turn in range(1, GROUPS)
+        ]
+
+    def ring_copies(buffer, number):
+        def move(owner, part, turn, order):
+            piece = buffer.at[owner, pl.ds(part * QUARTER, QUARTER)]
+            return pltpu.make_async_remote_copy(
+                src_ref=piece,
+                dst_ref=piece,
+                send_sem=send_sem.at[number + order],
+                recv_sem=recv_sem.at[number + order],
+                device_id=near_device(REACH, turn),
+                device_id_type=MESH,
+            )
+
+        right = [move(group, part, 1, part) for part in (0, 1, 2, 3)]
+        left = [move(group, part, 3, 4 + part) for part in (2, 3, 0, 1)]
+        starts = [copy for pair in zip(right, left) for copy in pair]
+        onward = []
+        for step in range(2):
+            onward.append(move(groups[3], step, 1, 8 + step))
+            onward.append(move(groups[1], step + 2, 3, 10 + step))
+        return starts, starts[:4], onward, starts[4:] + onward
+
+    def halo_copies(buffer, number):
+        return [
+            pltpu.make_async_remote_copy(
+                src_ref=buffer.at[:, 1],
+                dst_ref=buffer.at[:, PX + 1],
+                send_sem=send_sem.at[number],
+                recv_sem=recv_sem.at[number],
+                device_id=near_device(REACH - 1, 0),
+                device_id_type=MESH,
+            ),
+            pltpu.make_async_remote_copy(
+                src_ref=buffer.at[:, PX],
+                dst_ref=buffer.at[:, 0],
+                send_sem=send_sem.at[number + 1],
+                recv_sem=recv_sem.at[number + 1],
+                device_id=near_device(REACH + 1, 0),
+                device_id_type=MESH,
+            ),
+        ]
+
+    REQ, ROWS, ROWS2, HEAT, HEAT2, TARGET = 0, 1, 2, 3, 4, 5
+    HALO, HALO2 = 6, 8
+    GATHER, GATHER2, SHARE, SHARE2, VEE, VEE2 = 10, 14, 26, 30, 34, 38
+
+    far_send(req_out, req_in, REQ)
+
+    for load in loads[:2] + loads[3:]:
+        load.wait()
+
     key_lane = iota((COLS, FAR), 1)
     take_own = jnp.where(key_lane + partner * FAR == key_down, 1.0, 0.0).astype(BF16)
     row_all = iota((GROUPS * FAR, COLS), 0)
@@ -228,137 +361,6 @@
 
     warm = conduct(temp[...])
     cold_parts, warm_parts = stacked(temp[...]), stacked(warm)
-
-    pl.semaphore_wait(
-        barrier, NEAR * GROUPS - 1 + jnp.where(inside, BLOCK - 1, BLOCK).astype(jnp.int32)
-    )
-
-    def far_copy(source, target, index, number):
-        return pltpu.make_async_remote_copy(
-            src_ref=source.at[index],
-            dst_ref=target.at[place],
-            send_sem=send_sem.at[number],
-            recv_sem=recv_sem.at[number],
-            device_id=far_device(index),
-            device_id_type=MESH,
-        )
-
-    def far_send(source, target, number):
-        def one(order, _):
-            far_copy(source, target, far_index(order), number).start()
-            return 0
-
-        lax.fori_loop(0, BLOCK - 1, one, 0)
-
-        @pl.when(jnp.logical_not(inside))
-        def _():
-            one(BLOCK - 1, 0)
-
-        @pl.when(inside)
-        def _():
-            target[place] = source[place]
-
-    def far_done(buffer, sem, number):
-        @pl.when(inside)
-        def _():
-            part = buffer.at[pl.ds(0, BLOCK - 1)]
-            pltpu.make_async_copy(part, part, sem.at[number]).wait()
-
-        @pl.when(jnp.logical_not(inside))
-        def _():
-            pltpu.make_async_copy(buffer, buffer, sem.at[number]).wait()
-
-    def heat_send(source, target, number):
-        for offset, turn in near_order:
-            pltpu.make_async_remote_copy(
-                src_ref=source.at[offset],
-                dst_ref=target.at[offset * GROUPS + group],
-                send_sem=send_sem.at[number],
-                recv_sem=recv_sem.at[number],
-                device_id=near_device(offset, turn),
-                device_id_type=MESH,
-            ).start()
-        target[REACH * GROUPS + group] = source[REACH]
-
-    def heat_done(buffer, sem, number):
-        part = buffer.at[pl.ds(0, NEAR * GROUPS - 1)]
-        pltpu.make_async_copy(part, part, sem.at[number]).wait()
-
-    def target_send(number):
-        for offset in (0, 6, 1, 5, 2, 4):
-            pltpu.make_async_remote_copy(
-                src_ref=target_out.at[offset],
-                dst_ref=target_in.at[offset],
-                send_sem=send_sem.at[number],
-                recv_sem=recv_sem.at[number],
-                device_id=near_device(offset, 0),
-                device_id_type=MESH,
-            ).start()
-        target_in[REACH] = target_out[REACH]
-
-    def target_done(buffer, sem, number):
-        part = buffer.at[pl.ds(0, NEAR - 1)]
-        pltpu.make_async_copy(part, part, sem.at[number]).wait()
-
-    def group_copies(source_of, target_of, number):
-        return [
-            pltpu.make_async_remote_copy(
-                src_ref=source_of(turn),
-                dst_ref=target_of(turn),
-                send_sem=send_sem.at[number + turn],
-                recv_sem=recv_sem.at[number + turn],
-                device_id=near_device(REACH, turn),
-                device_id_type=MESH,
-            )
-            for turn in range(1, GROUPS)
-        ]
-
-    def ring_copies(buffer, number):
-        def move(owner, part, turn, order):
-            piece = buffer.at[owner, pl.ds(part * QUARTER, QUARTER)]
-            return pltpu.make_async_remote_copy(
-                src_ref=piece,
-                dst_ref=piece,
-                send_sem=send_sem.at[number + order],
-                recv_sem=recv_sem.at[number + order],
-                device_id=near_device(REACH, turn),
-                device_id_type=MESH,
-            )
-
-        right = [move(group, part, 1, part) for part in (0, 1, 2, 3)]
-        left = [move(group, part, 3, 4 + part) for part in (2, 3, 0, 1)]
-        starts = [copy for pair in zip(right, left) for copy in pair]
-        onward = []
-        for step in range(2):
-            onward.append(move(groups[3], step, 1, 8 + step))
-            onward.append(move(groups[1], step + 2, 3, 10 + step))
-        return starts, starts[:4], onward, starts[4:] + onward
-
-    def halo_copies(buffer, number):
-        return [
-            pltpu.make_async_remote_copy(
-                src_ref=buffer.at[:, 1],
-                dst_ref=buffer.at[:, PX + 1],
-                send_sem=send_sem.at[number],
-                recv_sem=recv_sem.at[number],
-                device_id=near_device(REACH - 1, 0),
-                device_id_type=MESH,
-            ),
-            pltpu.make_async_remote_copy(
-                src_ref=buffer.at[:, PX],
-                dst_ref=buffer.at[:, 0],
-                send_sem=send_sem.at[number + 1],
-                recv_sem=recv_sem.at[number + 1],
-                device_id=near_device(REACH + 1, 0),
-                device_id_type=MESH,
-            ),
-        ]
-
-    REQ, ROWS, ROWS2, HEAT, HEAT2, TARGET = 0, 1, 2, 3, 4, 5
-    HALO, HALO2 = 6, 8
-    GATHER, GATHER2, SHARE, SHARE2, VEE, VEE2 = 10, 14, 26, 30, 34, 38
-
-    far_send(req_out, req_in, REQ)
     target_send(TARGET)
     halos = halo_copies(cells, HALO)
     vees = group_copies(lambda turn: own_v.at[turn], lambda turn: all_v.at[turn], VEE)

time: 58.4 us -> 58 us (level)
  no operation moved by 1% of the time
where the time goes in v5:
time: 58 us; the launch traced here: 57.9 us
  Pallas kernels  57.2 us (99%)
  between operations  0.64 us (1%)
    pallas_call x1, Pallas kernels, on_device(): pl.pallas_call(kernel, out_shape=(jax.ShapeDtypeStruct((CH, COLS, NZ), F3...  55.4 us
    pallas_call x1, Pallas kernels, on_device(): pl.pallas_call(place_results, out_shape=(jax.ShapeDtypeStruct(new.shape,...  1.82 us

profile of v5, /device:TPU:1, one launch (start us, length us, event | category | flops | bytes accessed | tf_op | source)
XLA Modules:
  0.0 57.9 jit_solution(12986010755526078132)
XLA Ops:
  0.6 55.4 %solidify.1 = (f32[8,128,128]{2,1,0:T(8,128)}, f32[256,128]{1,0:T(8,128)}) custom-call(f32[8,8,16,128]{3,2,1,0:T(8,128)} %phases_hbm.1, f32[256,128]{1,0:T(8,128)} %temp_hbm.1, s32[1,128]{1,0:T(1,128)} %bitcast.4, s32[32]{0:T(128)} %bitcast.5, f32[4096]{0:T(1024)} %angle_hbm.1, f32[4096]{0:T(1024)} %melt_hbm.1, s32[16]{0:T(128)} %bitcast.6, s32[16]{0:T(128)} %local_hbm.1), custom_call_target="tpu_custom_call" | custom-call | tf_op jit(solution)/shard_map/solidify/pallas_call | solution.py:617
  56.0 1.8 %results.1 = (f32[8,128,128]{2,1,0:T(8,128)}, f32[256,128]{1,0:T(8,128)}) custom-call(f32[8,128,128]{2,1,0:T(8,128)} %get-tuple-element.6.new, f32[256,128]{1,0:T(8,128)} %get-tuple-element.7.temp), custom_call_target="tpu_custom_call" | custom-call | tf_op jit(solution)/shard_map/results/pallas_call | solution.py:656

commit v6 on v5

--- a/solution.py
+++ b/solution.py
@@ -130,25 +130,6 @@
     def near_device(offset, turn):
         return {"tile": near_tiles[offset], "ch": groups[turn]}
 
-    barrier = pltpu.get_barrier_semaphore()
-
-    def greet_far(number, _):
-        pl.semaphore_signal(
-            barrier, inc=1, device_id=far_device(far_index(number)), device_id_type=MESH
-        )
-        return 0
-
-    lax.fori_loop(0, BLOCK - 1, greet_far, 0)
-
-    @pl.when(jnp.logical_not(inside))
-    def _():
-        greet_far(BLOCK - 1, 0)
-
-    for offset, turn in near_order:
-        pl.semaphore_signal(
-            barrier, inc=1, device_id=near_device(offset, turn), device_id_type=MESH
-        )
-
     loads = [
         pltpu.make_async_copy(phases_hbm, cells.at[:, pl.ds(1, PX)], load_sem.at[0]),
         pltpu.make_async_copy(temp_hbm, temp, load_sem.at[1]),
@@ -159,7 +140,28 @@
         pltpu.make_async_copy(owner_hbm, owners, load_sem.at[6]),
         pltpu.make_async_copy(local_hbm, locals_, load_sem.at[7]),
     ]
-    for load in loads:
+    loads[2].start()
+
+    barrier = pltpu.get_barrier_semaphore()
+
+    def greet_far(number, _):
+        pl.semaphore_signal(
+            barrier, inc=1, device_id=far_device(far_index(number)), device_id_type=MESH
+        )
+        return 0
+
+    lax.fori_loop(0, BLOCK - 1, greet_far, 0)
+
+    @pl.when(jnp.logical_not(inside))
+    def _():
+        greet_far(BLOCK - 1, 0)
+
+    for offset, turn in near_order:
+        pl.semaphore_signal(
+            barrier, inc=1, device_id=near_device(offset, turn), device_id_type=MESH
+        )
+
+    for load in loads[:2] + loads[3:]:
         load.start()
     loads[2].wait()
 

time: 58 us -> 58 us (level)
  no operation moved by 1% of the time
where the time goes in v6:
time: 58 us; the launch traced here: 57.9 us
  Pallas kernels  57.2 us (99%)
  between operations  0.64 us (1%)
    pallas_call x1, Pallas kernels, on_device(): pl.pallas_call(kernel, out_shape=(jax.ShapeDtypeStruct((CH, COLS, NZ), F3...  55.4 us
    pallas_call x1, Pallas kernels, on_device(): pl.pallas_call(place_results, out_shape=(jax.ShapeDtypeStruct(new.shape,...  1.82 us

profile of v6, /device:TPU:1, one launch (start us, length us, event | category | flops | bytes accessed | tf_op | source)
XLA Modules:
  0.0 57.9 jit_solution(7367546815051228463)
XLA Ops:
  0.6 55.4 %solidify.1 = (f32[8,128,128]{2,1,0:T(8,128)}, f32[256,128]{1,0:T(8,128)}) custom-call(f32[8,8,16,128]{3,2,1,0:T(8,128)} %phases_hbm.1, f32[256,128]{1,0:T(8,128)} %temp_hbm.1, s32[1,128]{1,0:T(1,128)} %bitcast.4, s32[32]{0:T(128)} %bitcast.5, f32[4096]{0:T(1024)} %angle_hbm.1, f32[4096]{0:T(1024)} %melt_hbm.1, s32[16]{0:T(128)} %bitcast.6, s32[16]{0:T(128)} %local_hbm.1), custom_call_target="tpu_custom_call" | custom-call | tf_op jit(solution)/shard_map/solidify/pallas_call | solution.py:619
  56.0 1.8 %results.1 = (f32[8,128,128]{2,1,0:T(8,128)}, f32[256,128]{1,0:T(8,128)}) custom-call(f32[8,128,128]{2,1,0:T(8,128)} %get-tuple-element.6.new, f32[256,128]{1,0:T(8,128)} %get-tuple-element.7.temp), custom_call_target="tpu_custom_call" | custom-call | tf_op jit(solution)/shard_map/results/pallas_call | solution.py:658
